TPU v7x, 32 devices: a whole 2x2x4 slice. The times are simulated.
32 devices in a mesh: seq: 8 (over z, y), opt: 4 (over x, core).
Axes of the slice: x: 2, y: 2, z: 4, core: 2. Of those that a mesh axis runs over, the one named last changes fastest.
Arguments:
- inputs: bfloat16 [4, 1024, 512], P('opt', 'seq'), may hold values from -6 to 6
- cotangent: bfloat16 [4, 1024, 512], P('opt', 'seq'), may hold values from -6 to 6
- seq_lengths: int32 [4, 8], P('opt'), may hold values from 0 to 1024, as said below
- unit_slot: int32 [24], replicated, may hold values from 0 to 23, each once
- masters: float32 [24, 512, 512], P('opt', 'seq'), may hold values from -0.25 to 0.25
- first_moment: float32 [24, 512, 512], P('opt', 'seq'), may hold values from -6 to 6
- second_moment: float32 [24, 512, 512], P('opt', 'seq'), may hold values from 18.432 to 73.728
- bases: float32 [24, 2, 512, 512], P('opt', None, 'seq'), may hold values from -1 to 1, as said below
- stats: float32 [24, 2, 512, 512], P('opt', None, 'seq'), as said below
- vec_master: float32 [9216], P(('seq', 'opt')), may hold values from -1.5 to 1.5, as said below
- vec_first: float32 [9216], P(('seq', 'opt')), may hold values from -6 to 6
- vec_second: float32 [9216], P(('seq', 'opt')), may hold values from 20.48 to 81.92
Outputs:
- outputs: bfloat16 [4, 1024, 512], P('opt', 'seq')
- input_grad: float32 [4, 1024, 512], P('opt', 'seq')
- new_masters: float32 [24, 512, 512], P('opt', 'seq')
- new_first: float32 [24, 512, 512], P('opt', 'seq')
- new_second: float32 [24, 512, 512], P('opt', 'seq')
- new_bases: float32 [24, 2, 512, 512], P('opt', None, 'seq')
- new_stats: float32 [24, 2, 512, 512], P('opt', None, 'seq')
- new_vectors: float32 [9216], P(('seq', 'opt'))
- new_vec_first: float32 [9216], P(('seq', 'opt'))
- new_vec_second: float32 [9216], P(('seq', 'opt'))
Inputs may be any that keep to these rules, and one draw needn't show every extreme that they name: seq_lengths[r, j] is the length of the sequence that starts at device j of row r, 0 where none starts; sequences cover a power of two of devices, start at a multiple of it, have 1024 tokens or more (one device at the least) and 1024 at the most, and fill the row; some sequence of every draw has 1024 tokens. `unit_slot`: slot s belongs to opt index s // 6. `bases`: every [512, 512] matrix is orthogonal. `stats`: every [512, 512] matrix is symmetric with a positive diagonal that exceeds each row's other entries in absolute sum. `vec_master`: the 4608 entries of a layer are g1, c1, g2, c2, b_up, b_down.
All inputs are finite; a program needn't handle non-finite values.
Results may differ from a plain program's by a relative error of at most 0.014.
Values may be sent and summed in bfloat16 or wider, within the bound.
No kernel may reach another device: no remote copies, remote signals or barrier semaphores. Data moves between devices by JAX's collectives and lax.ppermute only.
A program may use at most 192 MiB of HBM per device.

v0:
```python
import math

import jax
import jax.numpy as jnp
from jax import lax
from jax.sharding import PartitionSpec as P

HEADS = 8
FF = 2048
BLOCK = 16
LAYERS = 2
STEP = 10
MAX_LEN = 4096


HIGH = lax.Precision.HIGHEST
LN_TWO = math.log(2.0)
NEG_FILL = -1e30
NORM_EPS = 1e-05
ADAM_EPS = 1e-08
RATE_MATRIX = 0.03
RATE_VECTOR = 0.2
WEIGHT_DECAY = 0.01
BETA_ONE = 0.9
BETA_TWO = 0.95
BETA_STAT = 0.95


def partner(value, axis, apart):
    return lax.ppermute(value, axis, [(i, i ^ 1 << apart) for i in range(lax.axis_size(axis))])


def shortened(value):
    return jax.tree.map(lambda a: a.astype(jnp.bfloat16) if a.dtype == jnp.float32 else a, value)


def pair_mean(values):
    shaped = values.reshape((values.shape[0] // 2, 2) + values.shape[1:])
    return 0.5 * (shaped[:, 0] + shaped[:, 1])


def pair_spread(grads):
    return 0.5 * jnp.repeat(grads, 2, axis=0)


def flip_pairs(segments):
    shaped = segments.reshape((segments.shape[0] // 2, 2) + segments.shape[1:])
    return shaped[:, ::-1].reshape(segments.shape)


def seg_scores(queries, key_segs):
    seg_count = key_segs.shape[0]
    shaped = queries.reshape((seg_count, queries.shape[0] // seg_count) + queries.shape[1:])
    result = jnp.einsum("sqhe,skhe->sqhk", shaped, key_segs, preferred_element_type=jnp.float32)
    return result.reshape(queries.shape[0], queries.shape[1], key_segs.shape[1])


def seg_apply(weights, value_segs):
    seg_count = value_segs.shape[0]
    shaped = weights.reshape((seg_count, weights.shape[0] // seg_count) + weights.shape[1:])
    result = jnp.einsum("sqhk,skhe->sqhe", shaped, value_segs, preferred_element_type=jnp.float32)
    return result.reshape(weights.shape[0], weights.shape[1], value_segs.shape[3])


def seg_collect(weights, row_values, seg_count):
    w_shaped = weights.reshape((seg_count, weights.shape[0] // seg_count) + weights.shape[1:])
    r_shaped = row_values.reshape(
        (seg_count, row_values.shape[0] // seg_count) + row_values.shape[1:]
    )
    return jnp.einsum("sqhk,sqhe->skhe", w_shaped, r_shaped, preferred_element_type=jnp.float32)


def layer_norm(values, gain_vec, bias_vec):
    centre = jnp.mean(values, axis=-1, keepdims=True)
    centred = values - centre
    spread = jnp.mean(centred * centred, axis=-1, keepdims=True)
    return centred * lax.rsqrt(spread + NORM_EPS) * gain_vec + bias_vec


def gelu_exact(values):
    return jax.nn.gelu(values, approximate=False)


def make_groups(key_levels, value_levels, far_list, head_count, head_size, local_levels):

    def as_segs(row_values, seg_count):
        return row_values.reshape(seg_count, BLOCK, head_count, head_size)

    own_count = key_levels[0].shape[0] // BLOCK
    groups = [(as_segs(key_levels[0], own_count), as_segs(value_levels[0], own_count), 0.0, None)]
    for height in range(local_levels):
        seg_count = key_levels[height].shape[0] // BLOCK
        groups.append(
            (
                flip_pairs(as_segs(key_levels[height], seg_count)),
                flip_pairs(as_segs(value_levels[height], seg_count)),
                height * LN_TWO,
                None,
            )
        )
    for step_at, (far_keys, far_values, counted) in enumerate(far_list):
        groups.append(
            (
                as_segs(far_keys, 1),
                as_segs(far_values, 1),
                (local_levels + step_at) * LN_TWO,
                counted,
            )
        )
    return groups


def score_all(queries, groups, score_scale):
    parts = []
    for key_segs, value_segs, offset, counted in groups:
        piece = seg_scores(queries, key_segs) * score_scale + offset
        if counted is not None:
            piece = jnp.where(counted, piece, NEG_FILL)
        parts.append(piece)
    return jnp.concatenate(parts, axis=2)


def attend(queries, groups, score_scale):
    scores = score_all(queries, groups, score_scale)
    highest = jnp.max(scores, axis=2, keepdims=True)
    expo = jnp.exp(scores - highest)
    totals = jnp.sum(expo, axis=2, keepdims=True)
    probs = (expo / totals).astype(jnp.bfloat16)
    result = jnp.zeros(queries.shape, jnp.float32)
    for position, group in enumerate(groups):
        result = result + seg_apply(
            probs[:, :, BLOCK * position : BLOCK * (position + 1)], group[1]
        )
    return (result, highest[..., 0] + jnp.log(totals[..., 0]))


def attend_back(queries, groups, score_scale, log_total, out_grad):
    scores = score_all(queries, groups, score_scale)
    probs = jnp.exp(scores - log_total[..., None])
    prob_grad = jnp.concatenate([seg_scores(out_grad, group[1]) for group in groups], axis=2)
    inner = jnp.sum(probs * prob_grad, axis=2, keepdims=True)
    score_grad = (probs * (prob_grad - inner)).astype(jnp.bfloat16)
    probs_low = probs.astype(jnp.bfloat16)
    query_grad = jnp.zeros(queries.shape, jnp.float32)
    key_grads = []
    value_grads = []
    for position, (key_segs, value_segs, offset, counted) in enumerate(groups):
        piece = score_grad[:, :, BLOCK * position : BLOCK * (position + 1)]
        weights = probs_low[:, :, BLOCK * position : BLOCK * (position + 1)]
        query_grad = query_grad + seg_apply(piece, key_segs) * score_scale
        key_grads.append(seg_collect(piece, queries, key_segs.shape[0]) * score_scale)
        value_grads.append(seg_collect(weights, out_grad, key_segs.shape[0]))
    return (query_grad, key_grads, value_grads)


def coarse_up(near_keys, near_values, seq_index, tree_bits, span_bits):
    far_list = []
    own_keys, own_values = (near_keys, near_values)
    for bit_at in range(tree_bits):
        far_keys, far_values = partner((own_keys, own_values), "seq", bit_at)
        far_list.append((far_keys, far_values, bit_at + 1 <= span_bits))
        if bit_at + 1 < tree_bits:
            upper = seq_index >> bit_at & 1 == 1
            joined_keys = jnp.where(
                upper, jnp.concatenate([far_keys, own_keys]), jnp.concatenate([own_keys, far_keys])
            )
            joined_values = jnp.where(
                upper,
                jnp.concatenate([far_values, own_values]),
                jnp.concatenate([own_values, far_values]),
            )
            own_keys = pair_mean(joined_keys.astype(jnp.float32)).astype(jnp.bfloat16)
            own_values = pair_mean(joined_values.astype(jnp.float32)).astype(jnp.bfloat16)
    return far_list


def coarse_down(far_grads, seq_index, tree_bits, model_width):
    key_above = None
    value_above = None
    for bit_at in reversed(range(tree_bits)):
        upper = seq_index >> bit_at & 1 == 1
        if key_above is None:
            own_key = jnp.zeros((BLOCK, model_width), jnp.float32)
            other_key = own_key
            own_value = own_key
            other_value = own_key
        else:
            spread_keys = pair_spread(key_above)
            spread_values = pair_spread(value_above)
            own_key = jnp.where(upper, spread_keys[BLOCK:], spread_keys[:BLOCK])
            other_key = jnp.where(upper, spread_keys[:BLOCK], spread_keys[BLOCK:])
            own_value = jnp.where(upper, spread_values[BLOCK:], spread_values[:BLOCK])
            other_value = jnp.where(upper, spread_values[:BLOCK], spread_values[BLOCK:])
        back_key, back_value = partner(
            (
                shortened(other_key + far_grads[bit_at][0]),
                shortened(other_value + far_grads[bit_at][1]),
            ),
            "seq",
            bit_at,
        )
        key_above = own_key + back_key
        value_above = own_value + back_value
    return (key_above, value_above)


def per_device(
    inputs,
    cotangent,
    seq_lengths,
    unit_slot,
    masters,
    first_moment,
    second_moment,
    bases,
    stats,
    vec_master,
    vec_first,
    vec_second,
):
    seq_count = lax.axis_size("seq")
    opt_count = lax.axis_size("opt")
    seq_index = lax.axis_index("seq")
    tok_count = inputs.shape[1]
    model_width = inputs.shape[2]
    own_slots = masters.shape[0]
    row_count = masters.shape[1]
    head_count = HEADS
    head_size = model_width // head_count
    score_scale = head_size ** (-0.5)
    ff_blocks = FF // model_width
    per_layer = 4 + 2 * ff_blocks
    vec_width = 5 * model_width + FF
    local_levels = (tok_count // BLOCK).bit_length() - 1
    long_devs = min(max(MAX_LEN // tok_count, 1), seq_count)
    tree_bits = long_devs.bit_length() - 1
    packed_units, packed_vecs = (
        lax.all_gather(masters.astype(jnp.bfloat16)[None], ("seq", "opt"), axis=0, tiled=True),
        lax.all_gather(vec_master.astype(jnp.bfloat16)[None], ("seq", "opt"), axis=0, tiled=True),
    )
    slot_weights = (
        packed_units.reshape(seq_count, opt_count, own_slots, row_count, model_width)
        .transpose(1, 2, 0, 3, 4)
        .reshape(opt_count * own_slots, seq_count * row_count, model_width)
    )
    units = jnp.take(slot_weights, unit_slot, axis=0)
    vectors = packed_vecs.reshape(-1).astype(jnp.float32)
    span_bits = jnp.zeros((), jnp.int32)
    for bit_at in range(tree_bits + 1):
        start_dev = seq_index >> bit_at << bit_at
        span_bits = jnp.where(
            seq_lengths[0, start_dev] == tok_count * (1 << bit_at), bit_at, span_bits
        )

    def layer_weights(layer_at):
        block_units = units[layer_at * per_layer : (layer_at + 1) * per_layer]
        w_qkv = block_units[0:3].transpose(1, 0, 2).reshape(model_width, 3 * model_width)
        w_up = block_units[4 : 4 + ff_blocks].transpose(1, 0, 2).reshape(model_width, FF)
        w_down = block_units[4 + ff_blocks :].reshape(FF, model_width)
        layer_vec = vectors[layer_at * vec_width : (layer_at + 1) * vec_width]
        vec_parts = (
            layer_vec[0:model_width],
            layer_vec[model_width : 2 * model_width],
            layer_vec[2 * model_width : 3 * model_width],
            layer_vec[3 * model_width : 4 * model_width],
            layer_vec[4 * model_width : 4 * model_width + FF],
            layer_vec[4 * model_width + FF :],
        )
        return (w_qkv, block_units[3], w_up, w_down, vec_parts)

    hidden = inputs[0].astype(jnp.float32)
    saved = []
    for layer_at in range(LAYERS):
        w_qkv, w_out, w_up, w_down, vec_parts = layer_weights(layer_at)
        gain_one, bias_one, gain_two, bias_two, bias_up, bias_down = vec_parts
        normed = layer_norm(hidden, gain_one, bias_one).astype(jnp.bfloat16)
        qkv = jnp.dot(normed, w_qkv, preferred_element_type=jnp.float32).astype(jnp.bfloat16)
        queries = qkv[:, :model_width].reshape(tok_count, head_count, head_size)
        key_levels = [qkv[:, model_width : 2 * model_width]]
        value_levels = [qkv[:, 2 * model_width :]]
        for height in range(local_levels):
            key_levels.append(pair_mean(key_levels[-1].astype(jnp.float32)).astype(jnp.bfloat16))
            value_levels.append(
                pair_mean(value_levels[-1].astype(jnp.float32)).astype(jnp.bfloat16)
            )
        far_list = coarse_up(
            key_levels[local_levels], value_levels[local_levels], seq_index, tree_bits, span_bits
        )
        groups = make_groups(
            key_levels, value_levels, far_list, head_count, head_size, local_levels
        )
        attended, log_total = attend(queries, groups, score_scale)
        mixed = attended.reshape(tok_count, model_width).astype(jnp.bfloat16)
        middle = hidden + jnp.dot(mixed, w_out, preferred_element_type=jnp.float32)
        normed_two = layer_norm(middle, gain_two, bias_two).astype(jnp.bfloat16)
        pre_act = jnp.dot(normed_two, w_up, preferred_element_type=jnp.float32) + bias_up
        activated = gelu_exact(pre_act).astype(jnp.bfloat16)
        saved.append(
            (
                hidden,
                normed,
                queries,
                key_levels,
                groups,
                log_total,
                mixed,
                middle,
                normed_two,
                pre_act,
                activated,
            )
        )
        hidden = middle + jnp.dot(activated, w_down, preferred_element_type=jnp.float32) + bias_down
    grad = cotangent[0].astype(jnp.float32)
    unit_grads = [None] * LAYERS
    vec_grads = [None] * LAYERS
    for layer_at in reversed(range(LAYERS)):
        w_qkv, w_out, w_up, w_down, vec_parts = layer_weights(layer_at)
        gain_one, bias_one, gain_two, bias_two, bias_up, bias_down = vec_parts
        (
            layer_in,
            normed,
            queries,
            key_levels,
            groups,
            log_total,
            mixed,
            middle,
            normed_two,
            pre_act,
            activated,
        ) = saved[layer_at]
        down_grad = grad.astype(jnp.bfloat16)
        grad_down_w = jnp.einsum(
            "tf,td->fd", activated, down_grad, preferred_element_type=jnp.float32
        )
        grad_bias_down = jnp.sum(grad, axis=0)
        act_grad = jnp.einsum("td,fd->tf", down_grad, w_down, preferred_element_type=jnp.float32)
        unused, gelu_back = jax.vjp(gelu_exact, pre_act)
        pre_grad = gelu_back(act_grad)[0].astype(jnp.bfloat16)
        grad_up_w = jnp.einsum(
            "td,tf->df", normed_two, pre_grad, preferred_element_type=jnp.float32
        )
        grad_bias_up = jnp.sum(pre_grad.astype(jnp.float32), axis=0)
        normed_grad = jnp.einsum("tf,df->td", pre_grad, w_up, preferred_element_type=jnp.float32)
        unused, norm_back = jax.vjp(layer_norm, middle, gain_two, bias_two)
        middle_grad, grad_gain_two, grad_bias_two = norm_back(normed_grad)
        middle_grad = middle_grad + grad
        branch_grad = middle_grad.astype(jnp.bfloat16)
        grad_out_w = jnp.einsum("td,te->de", mixed, branch_grad, preferred_element_type=jnp.float32)
        mixed_grad = (
            jnp.einsum("te,de->td", branch_grad, w_out, preferred_element_type=jnp.float32)
            .astype(jnp.bfloat16)
            .reshape(tok_count, head_count, head_size)
        )
        query_grad, key_grads, value_grads = attend_back(
            queries, groups, score_scale, log_total, mixed_grad
        )
        key_acc = [jnp.zeros(level_keys.shape, jnp.float32) for level_keys in key_levels]
        value_acc = [jnp.zeros(level_keys.shape, jnp.float32) for level_keys in key_levels]
        key_acc[0] = key_grads[0].reshape(tok_count, model_width)
        value_acc[0] = value_grads[0].reshape(tok_count, model_width)
        for height in range(local_levels):
            key_acc[height] = key_acc[height] + flip_pairs(key_grads[1 + height]).reshape(
                -1, model_width
            )
            value_acc[height] = value_acc[height] + flip_pairs(value_grads[1 + height]).reshape(
                -1, model_width
            )
        far_grads = [
            (
                key_grads[1 + local_levels + bit_at].reshape(BLOCK, model_width),
                value_grads[1 + local_levels + bit_at].reshape(BLOCK, model_width),
            )
            for bit_at in range(tree_bits)
        ]
        near_key_grad, near_value_grad = coarse_down(far_grads, seq_index, tree_bits, model_width)
        key_acc[local_levels] = key_acc[local_levels] + near_key_grad
        value_acc[local_levels] = value_acc[local_levels] + near_value_grad
        for height in range(local_levels, 0, -1):
            key_acc[height - 1] = key_acc[height - 1] + pair_spread(key_acc[height])
            value_acc[height - 1] = value_acc[height - 1] + pair_spread(value_acc[height])
        qkv_grad = jnp.concatenate(
            [
                query_grad.reshape(tok_count, model_width).astype(jnp.bfloat16),
                key_acc[0].astype(jnp.bfloat16),
                value_acc[0].astype(jnp.bfloat16),
            ],
            axis=1,
        )
        grad_qkv_w = jnp.einsum("td,te->de", normed, qkv_grad, preferred_element_type=jnp.float32)
        normed_one_grad = jnp.einsum(
            "te,de->td", qkv_grad, w_qkv, preferred_element_type=jnp.float32
        )
        unused, norm_back_one = jax.vjp(layer_norm, layer_in, gain_one, bias_one)
        in_grad, grad_gain_one, grad_bias_one = norm_back_one(normed_one_grad)
        grad = in_grad + middle_grad
        unit_grads[layer_at] = jnp.concatenate(
            [
                grad_qkv_w.reshape(model_width, 3, model_width).transpose(1, 0, 2),
                grad_out_w[None],
                grad_up_w.reshape(model_width, ff_blocks, model_width).transpose(1, 0, 2),
                grad_down_w.reshape(ff_blocks, model_width, model_width),
            ],
            axis=0,
        )
        vec_grads[layer_at] = jnp.concatenate(
            [
                grad_gain_one,
                grad_bias_one,
                grad_gain_two,
                grad_bias_two,
                grad_bias_up,
                grad_bias_down,
            ]
        )
    all_units = jnp.concatenate(unit_grads, axis=0)
    all_vecs = jnp.concatenate(vec_grads)
    slot_grads = jnp.zeros_like(all_units).at[unit_slot].set(all_units)
    by_device = (
        slot_grads.reshape(opt_count, own_slots, seq_count, row_count, model_width)
        .transpose(2, 0, 1, 3, 4)
        .reshape(seq_count * opt_count, own_slots, row_count, model_width)
    )
    vec_device = all_vecs.reshape(seq_count * opt_count, -1)
    grad_units, grad_vecs = (
        lax.psum_scatter(by_device, ("seq", "opt"), scatter_dimension=0, tiled=True),
        lax.psum_scatter(vec_device, ("seq", "opt"), scatter_dimension=0, tiled=True),
    )
    grad_units = grad_units.reshape(own_slots, row_count, model_width)
    grad_vecs = grad_vecs.reshape(-1)
    packed_opt = jnp.concatenate([bases, grad_units[:, None]], axis=1)
    whole_opt = lax.all_gather(packed_opt.astype(jnp.bfloat16), "seq", axis=2, tiled=True).astype(
        packed_opt.dtype
    )
    left_full = whole_opt[:, 0]
    right_full = whole_opt[:, 1]
    grad_full = whole_opt[:, 2]
    row_start = seq_index * row_count
    left_cols = lax.dynamic_slice_in_dim(left_full, row_start, row_count, 2)
    grad_cols = lax.dynamic_slice_in_dim(grad_full, row_start, row_count, 2)
    rotated = jnp.einsum("sri,src->sic", left_cols, grad_full, precision=HIGH)
    rotated = jnp.einsum("sic,scd->sid", rotated, right_full, precision=HIGH)
    new_first = BETA_ONE * first_moment + (1.0 - BETA_ONE) * rotated
    new_second = BETA_TWO * second_moment + (1.0 - BETA_TWO) * rotated * rotated
    direction = (
        new_first
        / (1.0 - BETA_ONE**STEP)
        / (jnp.sqrt(new_second / (1.0 - BETA_TWO**STEP)) + ADAM_EPS)
    )
    turned_rows = jnp.einsum("sid,scd->sic", direction, right_full, precision=HIGH)
    turned_full = lax.all_gather(
        turned_rows.astype(jnp.bfloat16), "seq", axis=1, tiled=True
    ).astype(turned_rows.dtype)
    update = jnp.einsum("sri,sic->src", bases[:, 0], turned_full, precision=HIGH)
    new_masters = masters - RATE_MATRIX * (update + WEIGHT_DECAY * masters)
    left_stat = BETA_STAT * stats[:, 0] + (1.0 - BETA_STAT) * jnp.einsum(
        "src,sqc->srq", grad_units, grad_full, precision=HIGH
    )
    right_stat = BETA_STAT * stats[:, 1] + (1.0 - BETA_STAT) * jnp.einsum(
        "sqr,sqc->src", grad_cols, grad_full, precision=HIGH
    )
    new_stats = jnp.stack([left_stat, right_stat], axis=1)
    product = jnp.einsum("sprq,spqc->sprc", new_stats, whole_opt[:, 0:2], precision=HIGH)
    gram_part = jnp.einsum("sprc,sprd->spcd", product, product, precision=HIGH)
    gram = lax.psum(gram_part, "seq")
    factor = jnp.linalg.cholesky(gram)
    solved = lax.linalg.triangular_solve(
        factor, jnp.swapaxes(product, -1, -2), left_side=True, lower=True
    )
    new_bases = jnp.swapaxes(solved, -1, -2)
    new_vec_first = BETA_ONE * vec_first + (1.0 - BETA_ONE) * grad_vecs
    new_vec_second = BETA_TWO * vec_second + (1.0 - BETA_TWO) * grad_vecs * grad_vecs
    new_vectors = vec_master - RATE_VECTOR * (new_vec_first / (1.0 - BETA_ONE**STEP)) / (
        jnp.sqrt(new_vec_second / (1.0 - BETA_TWO**STEP)) + ADAM_EPS
    )
    return (
        hidden.astype(jnp.bfloat16)[None],
        grad[None],
        new_masters,
        new_first,
        new_second,
        new_bases,
        new_stats,
        new_vectors,
        new_vec_first,
        new_vec_second,
    )


def solution(mesh):
    placed = (
        P("opt", "seq", None),
        P("opt", "seq", None),
        P("opt", None),
        P(),
        P("opt", "seq", None),
        P("opt", "seq", None),
        P("opt", "seq", None),
        P("opt", None, "seq", None),
        P("opt", None, "seq", None),
        P(("seq", "opt")),
        P(("seq", "opt")),
        P(("seq", "opt")),
    )
    return jax.shard_map(
        per_device,
        mesh=mesh,
        in_specs=placed,
        out_specs=(
            P("opt", "seq", None),
            P("opt", "seq", None),
            P("opt", "seq", None),
            P("opt", "seq", None),
            P("opt", "seq", None),
            P("opt", None, "seq", None),
            P("opt", None, "seq", None),
            P(("seq", "opt")),
            P(("seq", "opt")),
            P(("seq", "opt")),
        ),
        check_vma=False,
    )
```

profile of v0, /device:TPU:11, one launch (start us, length us, event | category | flops | bytes accessed | tf_op | source)
XLA Modules:
  0.0 3256.0 jit_solution(5012785137584804686)
XLA Ops:
  13.5 40.0 %all-reduce.1 = bf16[9216]{0:T(1024)(128)(2,1)S(1)} all-reduce(bf16[9216]{0:T(1024)(128)(2,1)S(1)} %dynamic-update-slice.23), channel_id=2, replica_groups=mesh['seq'=8,'opt'=4] {'seq','opt'}, use_global_device_ids=true, to_apply=%add.1 | all-reduce | flops 9216 | bytes 36864
  58.2 50.9 %all-gather.10.cloned.1.call-done = bf16[192,64,512]{2,1,0:T(8,128)(2,1)} async-done(((bf16[6,64,512]{2,1,0:T(8,128)(2,1)}), bf16[192,64,512]{2,1,0:T(8,128)(2,1)}) %all-gather.10.cloned.1.call-update) | async-done | bytes 12582928 | tf_op jit(solution)/shard_map/all_gather | solution.py:238
  109.1 10.7 copy.2400
  119.8 10.7 gather_fusion
  130.5 6.5 broadcast_select_fusion
  137.1 4.6 copy-done
  149.8 5.8 slice_bitcast_fusion.3
  250.4 4.5 multiply_convert_fusion.1
  416.2 4.3 fusion.121
  494.7 3.9 fusion.437
  677.8 3.9 fusion.436
  792.1 11.5 broadcast_in_dim.237
  803.6 45.0 %scatter_fusion = f32[24,512,512]{2,1,0:T(8,128)} fusion(f32[24,512,512]{2,1,0:T(8,128)} %broadcast_in_dim.237, s32[24]{0:T(128)S(1)} %copy-done.185, f32[24,512,512]{2,1,0:T(8,128)} %convolution_dynamic-update-slice_fusion), kind=kCustom, calls=%fused_computation.1 | custom fusion | bytes 75497568 | tf_op jit(solution)/shard_map/scatter | solution.py:419
  848.6 17.9 copy.2625
  866.6 250.5 %reduce-scatter.2.cloned.1.call-done = f32[1,6,64,512]{3,2,1,0:T(8,128)} async-done(((f32[32,6,64,512]{3,2,1,0:T(8,128)}), f32[1,6,64,512]{3,2,1,0:T(8,128)}) %reduce-scatter.2.cloned.1.call-update) | async-done | bytes 786448 | tf_op jit(solution)/shard_map/reduce_scatter | solution.py:427
  1120.0 135.8 %all-gather.6.cloned.1.call-done = bf16[6,3,512,512]{3,2,0,1:T(8,128)(2,1)} async-done(((bf16[6,3,64,512]{3,2,0,1:T(8,128)(2,1)}), bf16[6,3,512,512]{3,2,0,1:T(8,128)(2,1)}) %all-gather.6.cloned.1.call-update) | async-done | bytes 9437200 | tf_op jit(solution)/shard_map/all_gather | solution.py:433
  1255.8 3.8 fusion.453
  1271.3 4.9 fusion.42
  1276.5 6.1 fusion.3
  1282.6 12.4 fusion.479
  1297.1 5.0 fusion.86
  1319.4 44.1 %all-reduce.2 = f32[32,288]{1,0:T(8,128)S(1)} all-reduce(f32[32,288]{1,0:T(8,128)S(1)} %reshape.1872), channel_id=5, replica_groups=mesh['seq'=8,'opt'=4] {'seq','opt'}, use_global_device_ids=true, to_apply=%region_57.58.clone | all-reduce | flops 9216 | bytes 73728
  1366.7 5.1 fusion.56
  1371.8 357.8 %all-reduce.5.cloned.1.call-done = f32[6,2,512,512]{2,3,1,0:T(8,128)} async-done(((f32[6,2,512,512]{2,3,1,0:T(8,128)}), f32[6,2,512,512]{2,3,1,0:T(8,128)}) %all-reduce.5.cloned.1.call-update) | async-done | bytes 12582928 | tf_op jit(solution)/shard_map/psum | solution.py:466
  1729.6 12.8 copy.2634
  1742.4 9.5 fusion.2
  1751.9 4.6 copy-done.1
  1756.6 140.7 %custom-call.34 = f32[6,2,128,128]{3,2,1,0:T(8,128)S(1)} custom-call(f32[6,2,128,128]{3,2,1,0:T(8,128)S(1)} %cholesky.274), custom_call_target="Cholesky" | custom-call | tf_op jit(solution)/shard_map/jit(cholesky)/cholesky | solution.py:467
  1897.2 6.2 cholesky.234
  1903.5 118.7 %custom-call.35 = f32[6,2,1,128,128]{3,4,2,1,0:T(8,128)} custom-call(f32[6,2,1,128,128]{4,3,2,1,0:T(8,128)S(1)} %select_bitcast_fusion.2), custom_call_target="InvertDiagBlocksLowerTriangular" | custom-call | tf_op jit(solution)/shard_map/jit(cholesky)/cholesky | solution.py:467
  2022.2 5.5 constant_dynamic-update-slice_fusion.38
  2027.8 4.0 slice_subtract_fusion
  2034.1 141.4 %custom-call.36 = f32[6,2,128,128]{3,2,1,0:T(8,128)S(1)} custom-call(f32[6,2,128,128]{3,2,1,0:T(8,128)} %cholesky.278), custom_call_target="Cholesky" | custom-call | tf_op jit(solution)/shard_map/jit(cholesky)/cholesky | solution.py:467
  2177.0 119.7 %custom-call.37 = f32[6,2,1,128,128]{3,4,2,1,0:T(8,128)} custom-call(f32[6,2,1,128,128]{4,3,2,1,0:T(8,128)} %get-tuple-element.187), custom_call_target="InvertDiagBlocksLowerTriangular" | custom-call | tf_op jit(solution)/shard_map/jit(cholesky)/cholesky | solution.py:467
  2296.7 4.4 convolution_dynamic-update-slice_fusion.1
  2301.1 6.2 slice_subtract_fusion.1
  2309.3 142.2 %custom-call.38 = f32[6,2,128,128]{3,2,1,0:T(8,128)} custom-call(f32[6,2,128,128]{3,2,1,0:T(8,128)} %cholesky.283), custom_call_target="Cholesky" | custom-call | tf_op jit(solution)/shard_map/jit(cholesky)/cholesky | solution.py:467
  2454.0 119.5 %custom-call.39 = f32[6,2,1,128,128]{3,4,2,1,0:T(8,128)} custom-call(f32[6,2,1,128,128]{4,3,2,1,0:T(8,128)} %get-tuple-element.185), custom_call_target="InvertDiagBlocksLowerTriangular" | custom-call | tf_op jit(solution)/shard_map/jit(cholesky)/cholesky | solution.py:467
  2576.8 6.6 fusion.33
  2583.4 142.2 %custom-call.40 = f32[6,2,128,128]{3,2,1,0:T(8,128)} custom-call(f32[6,2,128,128]{3,2,1,0:T(8,128)} %fusion.33), custom_call_target="Cholesky" | custom-call | tf_op jit(solution)/shard_map/jit(cholesky)/cholesky | solution.py:467
  2729.6 11.0 select_select_fusion
  2740.6 18.4 while.1
  2741.3 4.0 bitcast_dynamic-update-slice_fusion.4
  2746.0 4.0 bitcast_dynamic-update-slice_fusion.4
  2750.6 4.0 bitcast_dynamic-update-slice_fusion.4
  2755.3 3.7 bitcast_dynamic-update-slice_fusion.4
  2759.0 473.3 %custom-call.41 = f32[6,2,4,128,128]{3,4,2,1,0:T(8,128)} custom-call(f32[6,2,4,128,128]{4,3,2,1,0:T(8,128)} %bitcast.1078), custom_call_target="InvertDiagBlocksLowerTriangular" | custom-call | tf_op jit(solution)/shard_map/triangular_solve | solution.py:468
  3242.1 5.1 fusion.71
  (1114 shorter events, 701.7 us)
Async XLA Ops:
  7.2 102.0 %all-gather.10.cloned.1.call-start = ((), (), s32[]{:S(2)}) async-start(), calls=%async_computation.5 | async-start | bytes 12976128 | tf_op jit(solution)/shard_map/all_gather | solution.py:238
  9.2 1108.0 %reduce-scatter.2.cloned.1.call-start = ((), (), s32[]{:S(2)}) async-start(), calls=%async_computation.1 | async-start | bytes 25952256 | tf_op jit(solution)/shard_map/reduce_scatter | solution.py:427
  55.2 90.0 %copy-start.150 = (f32[128]{0:T(128)}, f32[128]{0:T(128)S(1)}, u32[]{:S(2)}) copy-start(f32[128]{0:T(128)S(1)} %broadcast_multiply_fusion.3) | copy-start | bytes 1540
  56.3 63.5 %copy-start.186 = (f32[128]{0:T(128)}, f32[128]{0:T(128)S(1)}, u32[]{:S(2)}) copy-start(f32[128]{0:T(128)S(1)} %fusion.188) | copy-start | bytes 1540
  57.0 88.3 %copy-start.162 = (f32[128]{0:T(128)}, f32[128]{0:T(128)S(1)}, u32[]{:S(2)}) copy-start(f32[128]{0:T(128)S(1)} %fusion.420) | copy-start | bytes 1540
  58.2 87.1 %copy-start.135 = (f32[512]{0:T(512)}, f32[512]{0:T(512)S(1)}, u32[]{:S(2)}) copy-start(f32[512]{0:T(512)S(1)} %get-tuple-element.264) | copy-start | bytes 6148
  58.2 87.1 %copy-start.146 = (f32[512]{0:T(512)}, f32[512]{0:T(512)S(1)}, u32[]{:S(2)}) copy-start(f32[512]{0:T(512)S(1)} %get-tuple-element.263) | copy-start | bytes 6148
  149.8 32.7 %copy-start.34 = (bf16[4,32,8,64]{3,2,1,0:T(8,128)(2,1)}, bf16[4,32,8,64]{3,2,1,0:T(8,128)(2,1)S(1)}, u32[]{:S(2)}) copy-start(bf16[4,32,8,64]{3,2,1,0:T(8,128)(2,1)S(1)} %reshape_reshape.58) | copy-start | bytes 393220
  158.5 48.5 %collective-permute-start = (bf16[16,512]{1,0:T(8,128)(2,1)}, bf16[16,512]{1,0:T(8,128)(2,1)S(1)}, u32[]{:S(2)}, u32[]{:S(2)}) collective-permute-start(bf16[16,512]{1,0:T(8,128)(2,1)} %bitcast.958), channel_id=1, source_target_pairs={{0,4},{4,0},{8,12},{12,8},{16,20},{20,16},{24,28},{28,24},{1,5},{5... | collective-permute-start | bytes 49160 | tf_op jit(solution)/shard_map/ppermute | solution.py:30
  181.3 25.7 collective-permute-start.3
  207.9 3.4 collective-permute-start.1
  209.0 3.5 collective-permute-start.4
  211.5 4.1 collective-permute-start.2
  213.2 31.9 collective-permute-start.5
  221.1 25.4 copy-start.32
  258.1 26.3 copy-start.55
  277.1 75.0 %collective-permute-start.6 = (bf16[16,512]{1,0:T(8,128)(2,1)}, bf16[16,512]{1,0:T(8,128)(2,1)S(1)}, u32[]{:S(2)}, u32[]{:S(2)}) collective-permute-start(bf16[16,512]{1,0:T(8,128)(2,1)} %bitcast.952), channel_id=1, source_target_pairs={{0,4},{4,0},{8,12},{12,8},{16,20},{20,16},{24,28},{28,24},{1,5},{5... | collective-permute-start | bytes 49160 | tf_op jit(solution)/shard_map/ppermute | solution.py:30
  286.2 25.9 copy-start.63
  310.9 43.6 %collective-permute-start.9 = (bf16[16,512]{1,0:T(8,128)(2,1)}, bf16[16,512]{1,0:T(8,128)(2,1)}, u32[]{:S(2)}, u32[]{:S(2)}) collective-permute-start(bf16[16,512]{1,0:T(8,128)(2,1)} %bitcast.949), channel_id=1, source_target_pairs={{0,4},{4,0},{8,12},{12,8},{16,20},{20,16},{24,28},{28,24},{1,5},{5... | collective-permute-start | bytes 49160 | tf_op jit(solution)/shard_map/ppermute | solution.py:30
  333.1 40.3 %copy-start.10 = (bf16[128,512]{0,1:T(8,128)(2,1)}, bf16[128,512]{0,1:T(8,128)(2,1)S(1)}, u32[]{:S(2)}) copy-start(bf16[128,512]{0,1:T(8,128)(2,1)S(1)} %copy.2457) | copy-start | bytes 393220
  353.7 5.4 collective-permute-start.7
  355.4 7.1 collective-permute-start.10
  361.5 8.4 collective-permute-start.8
  364.7 46.0 %collective-permute-start.11 = (bf16[16,512]{1,0:T(8,128)(2,1)}, bf16[16,512]{1,0:T(8,128)(2,1)}, u32[]{:S(2)}, u32[]{:S(2)}) collective-permute-start(bf16[16,512]{1,0:T(8,128)(2,1)} %bitcast.947), channel_id=1, source_target_pairs={{0,16},{4,20},{8,24},{12,28},{16,0},{20,4},{24,8},{28,12},{1,17},{... | collective-permute-start | bytes 49160 | tf_op jit(solution)/shard_map/ppermute | solution.py:30
  379.2 33.0 %copy-start.33 = (f32[8,64,128]{2,1,0:T(8,128)}, f32[8,64,128]{2,1,0:T(8,128)S(1)}, u32[]{:S(2)}) copy-start(f32[8,64,128]{2,1,0:T(8,128)S(1)} %fusion.334) | copy-start | bytes 786436
  516.5 80.6 %collective-permute-start.15 = (bf16[16,512]{1,0:T(8,128)(2,1)S(1)}, bf16[16,512]{1,0:T(8,128)(2,1)}, u32[]{:S(2)}, u32[]{:S(2)}) collective-permute-start(bf16[16,512]{1,0:T(8,128)(2,1)S(1)} %convert_element_type.649), channel_id=1, source_target_pairs={{0,16},{4,20},{8,24},{12,28},{16,0},{20,4},{24,8},{28,12},{1,17},{... | collective-permute-start | bytes 49160 | tf_op jit(solution)/shard_map/ppermute | solution.py:30
  542.6 59.5 %collective-permute-start.12 = (bf16[16,512]{1,0:T(8,128)(2,1)}, bf16[16,512]{1,0:T(8,128)(2,1)}, u32[]{:S(2)}, u32[]{:S(2)}) collective-permute-start(bf16[16,512]{1,0:T(8,128)(2,1)} %convert_element_type.638), channel_id=1, source_target_pairs={{0,16},{4,20},{8,24},{12,28},{16,0},{20,4},{24,8},{28,12},{1,17},{... | collective-permute-start | bytes 49160 | tf_op jit(solution)/shard_map/ppermute | solution.py:30
  587.4 27.6 copy-start.128
  587.4 32.1 copy-start.127
  589.4 34.8 %copy-start.118 = (f32[32,512]{1,0:T(8,128)S(1)}, f32[32,512]{1,0:T(8,128)}, u32[]{:S(2)}) copy-start(f32[32,512]{1,0:T(8,128)} %reshape_reshape.74) | copy-start | bytes 196612
  589.4 37.4 %copy-start.94 = (f32[64,512]{1,0:T(8,128)S(1)}, f32[64,512]{1,0:T(8,128)}, u32[]{:S(2)}) copy-start(f32[64,512]{1,0:T(8,128)} %reshape_reshape.73) | copy-start | bytes 393220
  601.2 11.0 collective-permute-start.16
  611.6 5.1 collective-permute-start.13
  616.3 6.4 collective-permute-start.17
  620.1 7.6 collective-permute-start.14
  684.7 30.1 collective-permute-start.21
  693.4 26.4 collective-permute-start.18
  718.9 11.0 collective-permute-start.22
  729.3 5.1 collective-permute-start.19
  734.1 11.0 collective-permute-start.23
  741.2 13.7 collective-permute-start.20
  866.6 251.8 %copy-start.25 = (f32[6,2,64,512]{3,2,1,0:T(8,128)S(1)}, f32[6,2,64,512]{3,2,1,0:T(8,128)}, u32[]{:S(2)}) copy-start(f32[6,2,64,512]{3,2,1,0:T(8,128)} %param.19) | copy-start | bytes 4718596
  866.6 389.2 %all-gather.6.cloned.1.call-start = ((), (), s32[]{:S(2)}) async-start(), calls=%async_computation.2 | async-start | bytes 10616832 | tf_op jit(solution)/shard_map/all_gather | solution.py:433
  1119.5 247.2 %all-gather.8.cloned.1.call-start = ((), (), s32[]{:S(2)}) async-start(), calls=%async_computation.3 | async-start | bytes 3538944 | tf_op jit(solution)/shard_map/all_gather | solution.py:452
  1268.9 460.6 %all-reduce.5.cloned.1.call-start = ((), (), s32[]{:S(2)}) async-start(), calls=%async_computation.4 | async-start | bytes 25165824 | tf_op jit(solution)/shard_map/psum | solution.py:466
  1302.2 62.6 %copy-start.24 = (f32[128,512]{1,0:T(8,128)S(1)}, f32[128,512]{1,0:T(8,128)}, u32[]{:S(2)}) copy-start(f32[128,512]{1,0:T(8,128)} %copy-done.22) | copy-start | bytes 786436
  2573.5 152.0 %copy-start.132 = (pred[128,128]{1,0:T(8,128)(4,1)S(1)}, pred[128,128]{1,0:T(8,128)(4,1)}, u32[]{:S(2)}) copy-start(pred[128,128]{1,0:T(8,128)(4,1)} %iota_compare_fusion.2) | copy-start | bytes 49156
  2576.8 152.8 %copy-start.64 = (pred[512,512]{1,0:T(8,128)(4,1)S(1)}, pred[512,512]{1,0:T(8,128)(4,1)}, u32[]{:S(2)}) copy-start(pred[512,512]{1,0:T(8,128)(4,1)} %iota_compare_fusion) | copy-start | bytes 786436
  (177 other events, 1268.0 us)
Sparse Core Ops, SparseCore 0:
  11.4 97.6 all-gather.9
  866.7 250.4 reduce-scatter.1
  1120.2 135.5 all-gather.5
  1269.1 59.7 all-gather.7
  1333.4 396.1 all-reduce.4
where the time goes:
time: 3280 us; the launch traced here: 3260 us
  other arithmetic  1520 us (46%)
  waiting for transfers between devices  795 us (24%)
  local copies, waits for them, and re-layouts  569 us (17%)
  matrix products  243 us (7%)
  blocking collectives  84.2 us (3%)
    another operation x18, other arithmetic, per_device(): factor = jnp.linalg.cholesky(gram)  932 us
    another operation x4, other arithmetic, per_device(): lax.linalg.triangular_solve(factor, jnp.swapaxes(product, -1, -2), left_s...  486 us
    psum x1, waiting for transfers between devices, per_device(): gram = lax.psum(gram_part, 'seq')  358 us
    reduce_scatter x1, waiting for transfers between devices, per_device(): lax.psum_scatter(by_device, ('seq', 'opt'), scatter_dimension=0, tiled=True)  251 us
    all_gather x1, waiting for transfers between devices, per_device(): lax.all_gather(packed_opt.astype(jnp.bfloat16), 'seq', axis=2, tiled=True)  136 us
    unnamed x2, blocking collectives  84.2 us
  transfers between devices with their start and end apart: 29, of which 4 were waited for; matrix products, arithmetic and copies ran while one was open for 14% of the time, Pallas kernels for 0%

commit v1 on v0

--- a/solution.py
+++ b/solution.py
@@ -1,8 +1,11 @@
+import functools
 import math
 
 import jax
 import jax.numpy as jnp
 from jax import lax
+from jax.experimental import pallas as pl
+from jax.experimental.pallas import tpu as pltpu
 from jax.sharding import PartitionSpec as P
 
 HEADS = 8
@@ -24,6 +27,289 @@
 BETA_ONE = 0.9
 BETA_TWO = 0.95
 BETA_STAT = 0.95
+
+PANEL = 8
+DIAG = 128
+VMEM_GRANT = 48 * 2**20
+IN_VMEM = pl.BlockSpec(memory_space=pltpu.VMEM)
+IN_SMEM = pl.BlockSpec(memory_space=pltpu.SMEM)
+
+
+def contract(left, right, left_dim, right_dim, precision=None):
+    return lax.dot_general(
+        left,
+        right,
+        (((left_dim,), (right_dim,)), ((), ())),
+        precision=precision,
+        preferred_element_type=jnp.float32,
+    )
+
+
+def split_two(values):
+    high = values.astype(jnp.bfloat16)
+    return (high, (values - high.astype(jnp.float32)).astype(jnp.bfloat16))
+
+
+def wide_left(left, right_low, left_dim, right_dim):
+    high, rest = split_two(left)
+    return contract(high, right_low, left_dim, right_dim) + contract(
+        rest, right_low, left_dim, right_dim
+    )
+
+
+def wide_right(left_low, right, left_dim, right_dim):
+    high, rest = split_two(right)
+    return contract(left_low, high, left_dim, right_dim) + contract(
+        left_low, rest, left_dim, right_dim
+    )
+
+
+def call_kernel(body, out_shapes, scratch, name, *operands, smem_count=0):
+    return pl.pallas_call(
+        body,
+        out_shape=out_shapes,
+        in_specs=[IN_SMEM] * smem_count + [IN_VMEM] * (len(operands) - smem_count),
+        out_specs=jax.tree.map(lambda _: IN_VMEM, out_shapes),
+        scratch_shapes=scratch,
+        compiler_params=pltpu.CompilerParams(vmem_limit_bytes=VMEM_GRANT),
+        name=name,
+    )(*operands)
+
+
+def eliminate(left_part, right_part, turn):
+    width = left_part.shape[1]
+    turned = pltpu.roll(left_part, turn, 1)
+    row_at = lax.broadcasted_iota(jnp.int32, (PANEL, width), 0)
+    columns = [
+        jnp.broadcast_to(turned[:, i : i + 1], (PANEL, width)) for i in range(PANEL)
+    ]
+    pivots = jnp.ones((PANEL, width), jnp.float32)
+    for i in range(PANEL):
+        pivot = jnp.broadcast_to(columns[i][i : i + 1, :], (PANEL, width))
+        factor = jnp.where(row_at > i, columns[i] * pltpu.reciprocal(pivot, approx=False), 0.0)
+        pivots = jnp.where(row_at == i, pivot, pivots)
+        left_part = left_part - factor * jnp.broadcast_to(left_part[i : i + 1, :], (PANEL, width))
+        right_part = right_part - factor * jnp.broadcast_to(
+            right_part[i : i + 1, :], (PANEL, width)
+        )
+        for j in range(i + 1, PANEL):
+            columns[j] = columns[j] - factor * jnp.broadcast_to(
+                columns[j][i : i + 1, :], (PANEL, width)
+            )
+    scale = lax.rsqrt(pivots)
+    return (left_part * scale, right_part * scale)
+
+
+def factorize(gram, upper, work, inverses):
+    count, size, _ = gram.shape
+    blocks = size // DIAG
+    eye = (
+        lax.broadcasted_iota(jnp.int32, (DIAG, DIAG), 0)
+        == lax.broadcasted_iota(jnp.int32, (DIAG, DIAG), 1)
+    ).astype(jnp.float32)
+    for block_at in range(blocks):
+        low, top = (block_at * DIAG, (block_at + 1) * DIAG)
+        for m in range(count):
+            work[m, :, 0:DIAG] = gram[m, low:top, low:top]
+            work[m, :, DIAG:] = eye
+
+        def panel(panel_at, carry):
+            row = pl.multiple_of(panel_at * PANEL, PANEL)
+            turn = lax.rem(DIAG - panel_at * PANEL, DIAG)
+            for m in range(count):
+                left_part, right_part = eliminate(
+                    work[m, pl.ds(row, PANEL), 0:DIAG], work[m, pl.ds(row, PANEL), DIAG:], turn
+                )
+                inverses[m, block_at, pl.ds(row, PANEL), :] = right_part
+                both = jnp.concatenate([left_part, right_part], axis=1)
+                work[m] = work[m] - contract(left_part, both, 0, 0, HIGH)
+            return carry
+
+        lax.fori_loop(0, DIAG // PANEL, panel, 0)
+        for m in range(count):
+            if block_at + 1 < blocks:
+                right_of = contract(inverses[m, block_at], gram[m, low:top, top:], 1, 0, HIGH)
+                upper[m, low:top, top:] = right_of
+                for other in range(block_at + 1, blocks):
+                    skip = (other - block_at - 1) * DIAG
+                    gram[m, other * DIAG : (other + 1) * DIAG, other * DIAG :] -= contract(
+                        right_of[:, skip : skip + DIAG], right_of[:, skip:], 0, 0, HIGH
+                    )
+
+
+def renew_body(piece_count, *refs):
+    offset_ref, stat_ref, basis_ref = refs[:3]
+    piece_refs = refs[3 : 3 + piece_count]
+    product, gram, upper, work, inverses = refs[3 + piece_count :]
+    count, size, _ = stat_ref.shape
+    for m in range(count):
+        product[m] = wide_left(stat_ref[m], basis_ref[m], 1, 0)
+        gram[m] = contract(product[m], product[m], 0, 0, HIGH)
+    factorize(gram, upper, work, inverses)
+    for low in range(0, size, DIAG):
+        top = low + DIAG
+        for m in range(count):
+            rest = product[m, :, low:top]
+            if low:
+                rest = rest - contract(product[m, :, :low], upper[m, :low, low:top], 1, 0, HIGH)
+            product[m, :, low:top] = contract(rest, inverses[m, low // DIAG], 1, 1, HIGH)
+    rows = piece_refs[0].shape[1]
+    for piece_at in range(piece_count):
+        row = pl.multiple_of(offset_ref[piece_at], 8)
+        piece_refs[piece_at][...] = product[:, pl.ds(row, rows), :].astype(jnp.bfloat16)
+
+
+def renew_bases(offsets, new_stat, basis_low):
+    count, size, _ = new_stat.shape
+    piece_count = offsets.shape[0]
+    square = pltpu.VMEM((count, size, size), jnp.float32)
+    return call_kernel(
+        functools.partial(renew_body, piece_count),
+        [
+            jax.ShapeDtypeStruct((count, size // piece_count, size), jnp.bfloat16)
+            for _ in range(piece_count)
+        ],
+        [
+            square,
+            square,
+            square,
+            pltpu.VMEM((count, DIAG, 2 * DIAG), jnp.float32),
+            pltpu.VMEM((count, size // DIAG, DIAG, DIAG), jnp.float32),
+        ],
+        "renew_bases",
+        offsets,
+        new_stat,
+        basis_low,
+        smem_count=1,
+    )
+
+
+def pack_body(slot_ref, stats, bases, first, second, *piece_refs):
+    for piece_at, piece_ref in enumerate(piece_refs):
+        slot = slot_ref[piece_at]
+        piece_ref[0:2] = stats[slot].astype(jnp.bfloat16)
+        piece_ref[2:4] = bases[slot].astype(jnp.bfloat16)
+        piece_ref[4] = first[slot].astype(jnp.bfloat16)
+        piece_ref[5] = second[slot].astype(jnp.bfloat16)
+
+
+def rotate_body(piece_count, *refs):
+    offset_ref, grad_ref = refs[:2]
+    given = refs[2 : 2 + piece_count]
+    sent = refs[2 + piece_count : 2 + 2 * piece_count]
+    stat_ref, basis_ref, whole, results = refs[2 + 2 * piece_count :]
+    rows = given[0].shape[1]
+    for piece_at in range(piece_count):
+        row = pl.multiple_of(offset_ref[piece_at], 8)
+        whole[:, pl.ds(row, rows), :] = given[piece_at][...].astype(jnp.float32)
+    grad = grad_ref[...]
+    left = whole[2].astype(jnp.bfloat16)
+    right = whole[3].astype(jnp.bfloat16)
+    basis_ref[0] = left
+    basis_ref[1] = right
+    results[0] = contract(grad, grad, 1, 1)
+    results[1] = contract(grad, grad, 0, 0)
+    stat_ref[0] = BETA_STAT * whole[0] + (1.0 - BETA_STAT) * results[0]
+    stat_ref[1] = BETA_STAT * whole[1] + (1.0 - BETA_STAT) * results[1]
+    rotated = wide_left(contract(left, grad, 0, 0), right, 1, 0)
+    results[2] = rotated
+    new_first = BETA_ONE * whole[4] + (1.0 - BETA_ONE) * rotated
+    new_second = BETA_TWO * whole[5] + (1.0 - BETA_TWO) * rotated * rotated
+    direction = (
+        new_first
+        / (1.0 - BETA_ONE**STEP)
+        / (jnp.sqrt(new_second / (1.0 - BETA_TWO**STEP)) + ADAM_EPS)
+    )
+    results[3] = wide_right(left, wide_left(direction, right, 1, 1), 1, 0)
+    for piece_at in range(piece_count):
+        row = pl.multiple_of(offset_ref[piece_at], 8)
+        sent[piece_at][...] = results[:, pl.ds(row, rows), :].astype(jnp.bfloat16)
+
+
+def rotate_slot(offsets, grad, pieces):
+    size = grad.shape[0]
+    piece_count = offsets.shape[0]
+    return call_kernel(
+        functools.partial(rotate_body, piece_count),
+        [
+            jax.ShapeDtypeStruct((4, size // piece_count, size), jnp.bfloat16)
+            for _ in range(piece_count)
+        ]
+        + [
+            jax.ShapeDtypeStruct((2, size, size), jnp.float32),
+            jax.ShapeDtypeStruct((2, size, size), jnp.bfloat16),
+        ],
+        [
+            pltpu.VMEM((6, size, size), jnp.float32),
+            pltpu.VMEM((4, size, size), jnp.float32),
+        ],
+        "rotate_slot",
+        offsets,
+        grad,
+        *pieces,
+        smem_count=1,
+    )
+
+
+def finish_body(own_slots, piece_count, *refs):
+    slot_ref, masters, first, second, stats = refs[:5]
+    given = refs[5 : 5 + piece_count]
+    new_masters, new_first, new_second, new_stats = refs[5 + piece_count :]
+    for piece_at in range(piece_count):
+        slot = slot_ref[piece_at]
+
+        @pl.when(slot < own_slots)
+        def _():
+            piece = given[piece_at]
+            rotated = piece[2].astype(jnp.float32)
+            update = piece[3].astype(jnp.float32)
+            new_first[slot] = BETA_ONE * first[slot] + (1.0 - BETA_ONE) * rotated
+            new_second[slot] = BETA_TWO * second[slot] + (1.0 - BETA_TWO) * rotated * rotated
+            new_masters[slot] = masters[slot] - RATE_MATRIX * (
+                update + WEIGHT_DECAY * masters[slot]
+            )
+            new_stats[slot] = BETA_STAT * stats[slot] + (1.0 - BETA_STAT) * piece[
+                0:2
+            ].astype(jnp.float32)
+
+
+def place_body(own_slots, slot_ref, *refs):
+    new_bases = refs[-1]
+    for piece_at, piece in enumerate(refs[:-1]):
+        slot = slot_ref[piece_at]
+
+        @pl.when(slot < own_slots)
+        def _():
+            new_bases[slot] = piece[...].astype(jnp.float32)
+
+
+def swap_pieces(pieces, axis):
+    device_count = lax.axis_size(axis)
+    return [pieces[0]] + [
+        lax.ppermute(pieces[k], axis, [(i, i ^ k) for i in range(device_count)])
+        for k in range(1, device_count)
+    ]
+
+
+def to_owners(pieces, axis, by_permutes):
+    if by_permutes:
+        return swap_pieces(pieces, axis)
+    stacked = jnp.stack(pieces)
+    device_count = lax.axis_size(axis)
+    padded = jnp.pad(stacked, [(0, device_count - len(pieces))] + [(0, 0)] * (stacked.ndim - 1))
+    swapped = lax.all_to_all(padded, axis, 0, 0, tiled=True)
+    kinds, _, width = pieces[0].shape
+    return [jnp.swapaxes(swapped, 0, 1).reshape(kinds, -1, width)]
+
+
+def to_homes(pieces, axis, by_permutes, own_slots):
+    if by_permutes:
+        return swap_pieces(pieces, axis)
+    kinds, _, width = pieces[0].shape
+    device_count = lax.axis_size(axis)
+    shaped = jnp.swapaxes(pieces[0].reshape(kinds, device_count, -1, width), 0, 1)
+    swapped = lax.all_to_all(shaped, axis, 0, 0, tiled=True)
+    return [swapped[slot] for slot in range(own_slots)]
 
 
 def partner(value, axis, apart):
@@ -234,6 +520,31 @@
     local_levels = (tok_count // BLOCK).bit_length() - 1
     long_devs = min(max(MAX_LEN // tok_count, 1), seq_count)
     tree_bits = long_devs.bit_length() - 1
+    size = seq_count * row_count
+    by_permutes = seq_count <= 8
+    if by_permutes:
+        relative = jnp.arange(seq_count, dtype=jnp.int32) ^ seq_index
+        offsets = relative * row_count
+        slot_at = relative
+    else:
+        offsets = jnp.zeros((1,), jnp.int32)
+        slot_at = jnp.arange(own_slots, dtype=jnp.int32)
+    packed_pieces = call_kernel(
+        pack_body,
+        [
+            jax.ShapeDtypeStruct((6, row_count, model_width), jnp.bfloat16)
+            for _ in range(slot_at.shape[0])
+        ],
+        [],
+        "pack_slots",
+        jnp.minimum(slot_at, own_slots - 1),
+        stats,
+        bases,
+        first_moment,
+        second_moment,
+        smem_count=1,
+    )
+    owner_pieces = to_owners(packed_pieces, "seq", by_permutes)
     packed_units, packed_vecs = (
         lax.all_gather(masters.astype(jnp.bfloat16)[None], ("seq", "opt"), axis=0, tiled=True),
         lax.all_gather(vec_master.astype(jnp.bfloat16)[None], ("seq", "opt"), axis=0, tiled=True),
@@ -417,58 +728,40 @@
     all_units = jnp.concatenate(unit_grads, axis=0)
     all_vecs = jnp.concatenate(vec_grads)
     slot_grads = jnp.zeros_like(all_units).at[unit_slot].set(all_units)
-    by_device = (
-        slot_grads.reshape(opt_count, own_slots, seq_count, row_count, model_width)
-        .transpose(2, 0, 1, 3, 4)
-        .reshape(seq_count * opt_count, own_slots, row_count, model_width)
-    )
     vec_device = all_vecs.reshape(seq_count * opt_count, -1)
-    grad_units, grad_vecs = (
-        lax.psum_scatter(by_device, ("seq", "opt"), scatter_dimension=0, tiled=True),
-        lax.psum_scatter(vec_device, ("seq", "opt"), scatter_dimension=0, tiled=True),
-    )
-    grad_units = grad_units.reshape(own_slots, row_count, model_width)
+    column_grads = lax.psum_scatter(
+        slot_grads.astype(jnp.bfloat16), "opt", scatter_dimension=0, tiled=True
+    )
+    column_grads = jnp.pad(column_grads, [(0, seq_count - own_slots), (0, 0), (0, 0)])
+    owner_grad = lax.psum_scatter(column_grads, "seq", scatter_dimension=0, tiled=True)[0]
+    grad_vecs = lax.psum_scatter(vec_device, ("seq", "opt"), scatter_dimension=0, tiled=True)
     grad_vecs = grad_vecs.reshape(-1)
-    packed_opt = jnp.concatenate([bases, grad_units[:, None]], axis=1)
-    whole_opt = lax.all_gather(packed_opt.astype(jnp.bfloat16), "seq", axis=2, tiled=True).astype(
-        packed_opt.dtype
-    )
-    left_full = whole_opt[:, 0]
-    right_full = whole_opt[:, 1]
-    grad_full = whole_opt[:, 2]
-    row_start = seq_index * row_count
-    left_cols = lax.dynamic_slice_in_dim(left_full, row_start, row_count, 2)
-    grad_cols = lax.dynamic_slice_in_dim(grad_full, row_start, row_count, 2)
-    rotated = jnp.einsum("sri,src->sic", left_cols, grad_full, precision=HIGH)
-    rotated = jnp.einsum("sic,scd->sid", rotated, right_full, precision=HIGH)
-    new_first = BETA_ONE * first_moment + (1.0 - BETA_ONE) * rotated
-    new_second = BETA_TWO * second_moment + (1.0 - BETA_TWO) * rotated * rotated
-    direction = (
-        new_first
-        / (1.0 - BETA_ONE**STEP)
-        / (jnp.sqrt(new_second / (1.0 - BETA_TWO**STEP)) + ADAM_EPS)
-    )
-    turned_rows = jnp.einsum("sid,scd->sic", direction, right_full, precision=HIGH)
-    turned_full = lax.all_gather(
-        turned_rows.astype(jnp.bfloat16), "seq", axis=1, tiled=True
-    ).astype(turned_rows.dtype)
-    update = jnp.einsum("sri,sic->src", bases[:, 0], turned_full, precision=HIGH)
-    new_masters = masters - RATE_MATRIX * (update + WEIGHT_DECAY * masters)
-    left_stat = BETA_STAT * stats[:, 0] + (1.0 - BETA_STAT) * jnp.einsum(
-        "src,sqc->srq", grad_units, grad_full, precision=HIGH
-    )
-    right_stat = BETA_STAT * stats[:, 1] + (1.0 - BETA_STAT) * jnp.einsum(
-        "sqr,sqc->src", grad_cols, grad_full, precision=HIGH
-    )
-    new_stats = jnp.stack([left_stat, right_stat], axis=1)
-    product = jnp.einsum("sprq,spqc->sprc", new_stats, whole_opt[:, 0:2], precision=HIGH)
-    gram_part = jnp.einsum("sprc,sprd->spcd", product, product, precision=HIGH)
-    gram = lax.psum(gram_part, "seq")
-    factor = jnp.linalg.cholesky(gram)
-    solved = lax.linalg.triangular_solve(
-        factor, jnp.swapaxes(product, -1, -2), left_side=True, lower=True
-    )
-    new_bases = jnp.swapaxes(solved, -1, -2)
+    *step_pieces, owner_stat, owner_basis = rotate_slot(offsets, owner_grad, owner_pieces)
+    home_pieces = to_homes(step_pieces, "seq", by_permutes, own_slots)
+    base_pieces = renew_bases(offsets, owner_stat, owner_basis)
+    whole_shape = jax.ShapeDtypeStruct(masters.shape, jnp.float32)
+    new_masters, new_first, new_second, new_stats = call_kernel(
+        functools.partial(finish_body, own_slots, len(home_pieces)),
+        [whole_shape, whole_shape, whole_shape, jax.ShapeDtypeStruct(stats.shape, jnp.float32)],
+        [],
+        "finish_slots",
+        slot_at,
+        masters,
+        first_moment,
+        second_moment,
+        stats,
+        *home_pieces,
+        smem_count=1,
+    )
+    (new_bases,) = call_kernel(
+        functools.partial(place_body, own_slots),
+        [jax.ShapeDtypeStruct(bases.shape, jnp.float32)],
+        [],
+        "place_bases",
+        slot_at,
+        *to_homes(base_pieces, "seq", by_permutes, own_slots),
+        smem_count=1,
+    )
     new_vec_first = BETA_ONE * vec_first + (1.0 - BETA_ONE) * grad_vecs
     new_vec_second = BETA_TWO * vec_second + (1.0 - BETA_TWO) * grad_vecs * grad_vecs
     new_vectors = vec_master - RATE_VECTOR * (new_vec_first / (1.0 - BETA_ONE**STEP)) / (

time: 3280 us -> 1380 us (0.42)
  other arithmetic: 1520 us -> 97.1 us
  waiting for transfers between devices: 795 us -> 332 us
  Pallas kernels: 0 us -> 113 us
  matrix products: 243 us -> 171 us
  local copies, waits for them, and re-layouts: 569 us -> 497 us
    another operation x26 -> x2, other arithmetic: 1420 us -> 1.83 us  [the longest x18 932 us: per_device(): factor = jnp.linalg.cholesky(gram)]
    psum x1 -> x0, waiting for transfers between devices: 358 us -> none  [per_device(): gram = lax.psum(gram_part, 'seq')]
    all_gather x2 -> x0, waiting for transfers between devices: 136 us -> none  [the longest x1 136 us: per_device(): lax.all_gather(packed_opt.astype(jnp.bfloat16), 'seq', axis=2, tiled=True)]
    ppermute x0 -> x21, waiting for transfers between devices: none -> 132 us  [swap_pieces(): lax.ppermute(pieces[k], axis, [(i, i ^ k) for i in range(device_count)])]
    pallas_call x0 -> x5, Pallas kernels: none -> 113 us  [call_kernel(): pl.pallas_call(body, out_shape=out_shapes, in_specs=[IN_SMEM] * smem_coun...]
    reduce_scatter x1 -> x2, waiting for transfers between devices: 251 us -> 147 us  [the longest x1 105 us: per_device(): lax.psum_scatter(slot_grads.astype(jnp.bfloat16), 'opt', scatter_dimensio...]
    another operation x13 -> x0, matrix products: 45.6 us -> none  [the longest x6 29.9 us: per_device(): factor = jnp.linalg.cholesky(gram)]
    dot_general x8 -> x0, matrix products: 37.2 us -> none  [the longest x1 12.4 us: per_device(): gram_part = jnp.einsum('sprc,sprd->spcd', product, product, precision=HIGH)]
  transfers between devices with their start and end apart: 29 -> 48, of which waited for: 4 -> 16; matrix products, arithmetic and copies ran while one was open for 14% -> 28% of each run, Pallas kernels for 0% -> 0%
where the time goes in v1:
time: 1380 us; the launch traced here: 1360 us
  local copies, waits for them, and re-layouts  497 us (36%)
  waiting for transfers between devices  332 us (24%)
  matrix products  171 us (12%)
  Pallas kernels  113 us (8%)
  other arithmetic  97.1 us (7%)
  blocking collectives  80.8 us (6%)
  starting transfers between devices  45.1 us (3%)
  between operations  18.7 us (1%)
    ppermute x21, waiting for transfers between devices, swap_pieces(): lax.ppermute(pieces[k], axis, [(i, i ^ k) for i in range(device_count)])  132 us
    pallas_call x5, Pallas kernels, call_kernel(): pl.pallas_call(body, out_shape=out_shapes, in_specs=[IN_SMEM] * smem_coun...  113 us
    reduce_scatter x1, waiting for transfers between devices, per_device(): lax.psum_scatter(slot_grads.astype(jnp.bfloat16), 'opt', scatter_dimensio...  105 us
    unnamed x2, blocking collectives  80.8 us
    unnamed x401, local copies, waits for them, and re-layouts  69.3 us
    all_gather x1, waiting for transfers between devices, per_device(): lax.all_gather(masters.astype(jnp.bfloat16)[None], ('seq', 'opt'), axis=0...  50.9 us
    scatter x1, local copies, waits for them, and re-layouts, per_device(): slot_grads = jnp.zeros_like(all_units).at[unit_slot].set(all_units)  44.9 us
    dot_general x28, matrix products, seg_apply(): jnp.einsum('sqhk,skhe->sqhe', shaped, value_segs, preferred_element_type=...  43.3 us
  transfers between devices with their start and end apart: 48, of which 16 were waited for; matrix products, arithmetic and copies ran while one was open for 28% of the time, Pallas kernels for 0%

profile of v1, /device:TPU:11, one launch (start us, length us, event | category | flops | bytes accessed | tf_op | source)
XLA Modules:
  0.0 1356.1 jit_solution(9129869765964294452)
XLA Ops:
  13.5 40.0 %all-reduce.1 = bf16[9216]{0:T(1024)(128)(2,1)S(1)} all-reduce(bf16[9216]{0:T(1024)(128)(2,1)S(1)} %dynamic-update-slice), channel_id=2, replica_groups=mesh['seq'=8,'opt'=4] {'seq','opt'}, use_global_device_ids=true, to_apply=%add.1 | all-reduce | flops 9216 | bytes 36864
  58.2 50.9 %all-gather.4.cloned.1.call-done = bf16[192,64,512]{2,1,0:T(8,128)(2,1)} async-done(((bf16[6,64,512]{2,1,0:T(8,128)(2,1)}), bf16[192,64,512]{2,1,0:T(8,128)(2,1)}) %all-gather.4.cloned.1.call-update) | async-done | bytes 12582928 | tf_op jit(solution)/shard_map/all_gather | solution.py:549
  109.1 10.7 copy.1737
  119.9 10.7 gather_fusion
  130.6 6.5 broadcast_select_fusion
  137.1 4.6 copy-done.27
  149.8 5.8 slice_bitcast_fusion
  189.6 2.6 copy.1779
  199.6 3.1 copy.1778
  247.4 5.4 multiply_convert_fusion.1
  432.4 5.2 fusion.56
  437.7 3.6 convert_reduce_fusion
  513.8 3.8 fusion.335
  604.3 5.3 copy.1961
  635.7 2.5 multiply_reduce_fusion.3
  676.4 3.4 fusion.172
  679.9 3.9 fusion.334
  683.8 2.7 fusion.212
  715.9 5.3 copy.1951
  750.4 3.5 bitcast_dynamic-update-slice_fusion.3
  753.9 2.7 fusion.3
  756.6 2.6 bitcast_dynamic-update-slice_fusion.1
  760.3 2.5 constant_dynamic-update-slice_fusion.22
  767.1 2.5 bitcast_dynamic-update-slice_fusion
  769.5 2.7 convolution_dynamic-update-slice_fusion
  772.2 11.5 broadcast_in_dim.233
  783.8 44.9 %scatter_fusion = f32[24,512,512]{2,1,0:T(8,128)} fusion(f32[24,512,512]{2,1,0:T(8,128)} %broadcast_in_dim.233, s32[24]{0:T(128)S(1)} %copy-done.169, f32[24,512,512]{2,1,0:T(8,128)} %convolution_dynamic-update-slice_fusion), kind=kCustom, calls=%fused_computation.1 | custom fusion | bytes 75497568 | tf_op jit(solution)/shard_map/scatter | solution.py:730
  828.7 13.2 convert_element_type.685
  842.5 105.4 %reduce-scatter.3.cloned.1.call-done = bf16[6,512,512]{2,1,0:T(8,128)(2,1)} async-done(((bf16[24,512,512]{2,1,0:T(8,128)(2,1)}), bf16[6,512,512]{2,1,0:T(8,128)(2,1)}) %reduce-scatter.3.cloned.1.call-update) | async-done | bytes 3145744 | tf_op jit(solution)/shard_map/reduce_scatter | solution.py:732
  947.8 4.3 pad.4
  952.2 3.4 pack_slots.1
  963.1 5.1 fusion.21
  976.5 16.8 %collective-permute-done.25.refs_4_ = bf16[6,64,512]{2,1,0:T(8,128)(2,1)S(1)} collective-permute-done((bf16[6,64,512]{2,1,0:T(8,128)(2,1)}, bf16[6,64,512]{2,1,0:T(8,128)(2,1)S(1)}, u32[]{:S(2)}, u32[]{:S(2)}) %collective-permute-start.25) | collective-permute-done | bytes 393248 | tf_op jit(solution)/shard_map/ppermute | solution.py:289
  999.7 9.6 collective-permute-done.26.refs_5_
  1009.3 4.9 collective-permute-done.28.refs_7_
  1014.2 36.6 %collective-permute-done.29.refs_8_ = bf16[6,64,512]{2,1,0:T(8,128)(2,1)S(1)} collective-permute-done((bf16[6,64,512]{2,1,0:T(8,128)(2,1)S(1)}, bf16[6,64,512]{2,1,0:T(8,128)(2,1)S(1)}, u32[]{:S(2)}, u32[]{:S(2)}) %collective-permute-start.29) | collective-permute-done | bytes 393248 | tf_op jit(solution)/shard_map/ppermute | solution.py:289
  1051.6 12.6 collective-permute-done.30.refs_9_
  1064.9 42.1 %reduce-scatter.5.cloned.1.call-done = bf16[1,512,512]{2,1,0:T(8,128)(2,1)} async-done(((bf16[8,512,512]{2,1,0:T(8,128)(2,1)}), bf16[1,512,512]{2,1,0:T(8,128)(2,1)}) %reduce-scatter.5.cloned.1.call-update) | async-done | bytes 524304 | tf_op jit(solution)/shard_map/reduce_scatter | solution.py:736
  1110.0 6.9 rotate_slot.1
  1124.0 97.0 %renew_bases.1 = (bf16[2,64,512]{2,1,0:T(8,128)(2,1)S(1)}, bf16[2,64,512]{2,1,0:T(8,128)(2,1)S(1)}, bf16[2,64,512]{2,1,0:T(8,128)(2,1)}, bf16[2,64,512]{2,1,0:T(...) custom-call(s32[8]{0:T(128)S(1)} %broadcast_multiply_fusion.refs_0_,, ...), custom_call_target="tpu_custom_call" | custom-call | tf_op jit(solution)/shard_map/renew_bases/pallas_call | solution.py:68
  1235.0 40.7 %all-reduce.2 = f32[32,288]{1,0:T(8,128)} all-reduce(f32[32,288]{1,0:T(8,128)} %reshape.1804), channel_id=6, replica_groups=mesh['seq'=8,'opt'=4] {'seq','opt'}, use_global_device_ids=true, to_apply=%region_49.50.clone | all-reduce | flops 9216 | bytes 73728
  1281.9 7.6 collective-permute-done.42.refs_5_
  1289.4 4.2 collective-permute-start.33
  1294.3 6.1 collective-permute-done.44.refs_7_
  1307.2 22.5 %collective-permute-done.35.refs_10_ = bf16[4,64,512]{2,1,0:T(8,128)(2,1)S(1)} collective-permute-done((bf16[4,64,512]{2,1,0:T(8,128)(2,1)}, bf16[4,64,512]{2,1,0:T(8,128)(2,1)S(1)}, u32[]{:S(2)}, u32[]{:S(2)}) %collective-permute-start.35) | collective-permute-done | bytes 262176 | tf_op jit(solution)/shard_map/ppermute | solution.py:289
  1329.6 8.0 collective-permute-done.36.refs_11_
  1337.6 7.0 collective-permute-done.37.refs_12_
  1345.8 3.6 finish_slots.1
  (1050 shorter events, 630.9 us)
Async XLA Ops:
  7.2 102.0 %all-gather.4.cloned.1.call-start = ((), (), s32[]{:S(2)}) async-start(), calls=%async_computation.4 | async-start | bytes 12976128 | tf_op jit(solution)/shard_map/all_gather | solution.py:549
  9.2 938.6 %reduce-scatter.3.cloned.1.call-start = ((), (), s32[]{:S(2)}) async-start(), calls=%async_computation.2 | async-start | bytes 15728640 | tf_op jit(solution)/shard_map/reduce_scatter | solution.py:732
  158.5 44.2 %collective-permute-start = (bf16[16,512]{1,0:T(8,128)(2,1)}, bf16[16,512]{1,0:T(8,128)(2,1)}, u32[]{:S(2)}, u32[]{:S(2)}) collective-permute-start(bf16[16,512]{1,0:T(8,128)(2,1)} %bitcast.809), channel_id=1, source_target_pairs={{0,4},{4,0},{8,12},{12,8},{16,20},{20,16},{24,28},{28,24},{1,5},{5... | collective-permute-start | bytes 49160 | tf_op jit(solution)/shard_map/ppermute | solution.py:316
  170.6 32.2 %collective-permute-start.3 = (bf16[16,512]{1,0:T(8,128)(2,1)}, bf16[16,512]{1,0:T(8,128)(2,1)}, u32[]{:S(2)}, u32[]{:S(2)}) collective-permute-start(bf16[16,512]{1,0:T(8,128)(2,1)} %bitcast.806), channel_id=1, source_target_pairs={{0,4},{4,0},{8,12},{12,8},{16,20},{20,16},{24,28},{28,24},{1,5},{5... | collective-permute-start | bytes 49160 | tf_op jit(solution)/shard_map/ppermute | solution.py:316
  203.7 4.1 collective-permute-start.1
  204.7 4.2 collective-permute-start.4
  208.0 4.1 collective-permute-start.2
  209.7 31.9 %collective-permute-start.5 = (bf16[16,512]{1,0:T(8,128)(2,1)}, bf16[16,512]{1,0:T(8,128)(2,1)}, u32[]{:S(2)}, u32[]{:S(2)}) collective-permute-start(bf16[16,512]{1,0:T(8,128)(2,1)} %bitcast.804), channel_id=1, source_target_pairs={{0,16},{4,20},{8,24},{12,28},{16,0},{20,4},{24,8},{28,12},{1,17},{... | collective-permute-start | bytes 49160 | tf_op jit(solution)/shard_map/ppermute | solution.py:316
  274.6 75.8 %collective-permute-start.6 = (bf16[16,512]{1,0:T(8,128)(2,1)}, bf16[16,512]{1,0:T(8,128)(2,1)}, u32[]{:S(2)}, u32[]{:S(2)}) collective-permute-start(bf16[16,512]{1,0:T(8,128)(2,1)} %bitcast.803), channel_id=1, source_target_pairs={{0,4},{4,0},{8,12},{12,8},{16,20},{20,16},{24,28},{28,24},{1,5},{5... | collective-permute-start | bytes 49160 | tf_op jit(solution)/shard_map/ppermute | solution.py:316
  305.3 50.4 %collective-permute-start.9 = (bf16[16,512]{1,0:T(8,128)(2,1)}, bf16[16,512]{1,0:T(8,128)(2,1)}, u32[]{:S(2)}, u32[]{:S(2)}) collective-permute-start(bf16[16,512]{1,0:T(8,128)(2,1)} %bitcast.800), channel_id=1, source_target_pairs={{0,4},{4,0},{8,12},{12,8},{16,20},{20,16},{24,28},{28,24},{1,5},{5... | collective-permute-start | bytes 49160 | tf_op jit(solution)/shard_map/ppermute | solution.py:316
  354.9 11.0 collective-permute-start.7
  360.3 11.1 collective-permute-start.10
  370.4 11.9 collective-permute-start.8
  375.9 51.4 %collective-permute-start.11 = (bf16[16,512]{1,0:T(8,128)(2,1)}, bf16[16,512]{1,0:T(8,128)(2,1)}, u32[]{:S(2)}, u32[]{:S(2)}) collective-permute-start(bf16[16,512]{1,0:T(8,128)(2,1)} %bitcast.798), channel_id=1, source_target_pairs={{0,16},{4,20},{8,24},{12,28},{16,0},{20,4},{24,8},{28,12},{1,17},{... | collective-permute-start | bytes 49160 | tf_op jit(solution)/shard_map/ppermute | solution.py:316
  536.1 73.5 %collective-permute-start.15 = (bf16[16,512]{1,0:T(8,128)(2,1)}, bf16[16,512]{1,0:T(8,128)(2,1)}, u32[]{:S(2)}, u32[]{:S(2)}) collective-permute-start(bf16[16,512]{1,0:T(8,128)(2,1)} %convert_element_type.648), channel_id=1, source_target_pairs={{0,16},{4,20},{8,24},{12,28},{16,0},{20,4},{24,8},{28,12},{1,17},{... | collective-permute-start | bytes 49160 | tf_op jit(solution)/shard_map/ppermute | solution.py:316
  562.0 50.5 %collective-permute-start.12 = (bf16[16,512]{1,0:T(8,128)(2,1)}, bf16[16,512]{1,0:T(8,128)(2,1)}, u32[]{:S(2)}, u32[]{:S(2)}) collective-permute-start(bf16[16,512]{1,0:T(8,128)(2,1)} %convert_element_type.637), channel_id=1, source_target_pairs={{0,16},{4,20},{8,24},{12,28},{16,0},{20,4},{24,8},{28,12},{1,17},{... | collective-permute-start | bytes 49160 | tf_op jit(solution)/shard_map/ppermute | solution.py:316
  611.7 3.8 collective-permute-start.16
  614.8 3.0 collective-permute-start.13
  616.2 4.0 collective-permute-start.17
  619.2 4.0 collective-permute-start.14
  686.6 34.6 %collective-permute-start.21 = (bf16[16,512]{1,0:T(8,128)(2,1)S(1)}, bf16[16,512]{1,0:T(8,128)(2,1)}, u32[]{:S(2)}, u32[]{:S(2)}) collective-permute-start(bf16[16,512]{1,0:T(8,128)(2,1)S(1)} %convert_element_type.675), channel_id=1, source_target_pairs={{0,16},{4,20},{8,24},{12,28},{16,0},{20,4},{24,8},{28,12},{1,17},{... | collective-permute-start | bytes 49160 | tf_op jit(solution)/shard_map/ppermute | solution.py:316
  696.8 26.5 %collective-permute-start.18 = (bf16[16,512]{1,0:T(8,128)(2,1)}, bf16[16,512]{1,0:T(8,128)(2,1)}, u32[]{:S(2)}, u32[]{:S(2)}) collective-permute-start(bf16[16,512]{1,0:T(8,128)(2,1)} %convert_element_type.664), channel_id=1, source_target_pairs={{0,16},{4,20},{8,24},{12,28},{16,0},{20,4},{24,8},{28,12},{1,17},{... | collective-permute-start | bytes 49160 | tf_op jit(solution)/shard_map/ppermute | solution.py:316
  722.6 2.9 collective-permute-start.22
  724.1 3.9 collective-permute-start.19
  726.9 5.6 collective-permute-start.23
  730.8 6.7 collective-permute-start.20
  842.0 264.9 %reduce-scatter.5.cloned.1.call-start = ((), (), s32[]{:S(2)}) async-start(), calls=%async_computation.3 | async-start | bytes 4718592 | tf_op jit(solution)/shard_map/reduce_scatter | solution.py:736
  957.0 18.2 %collective-permute-start.24 = (bf16[6,64,512]{2,1,0:T(8,128)(2,1)}, bf16[6,64,512]{2,1,0:T(8,128)(2,1)S(1)}, u32[]{:S(2)}, u32[]{:S(2)}) collective-permute-start(bf16[6,64,512]{2,1,0:T(8,128)(2,1)} %get-tuple-element.41), channel_id=1, source_target_pairs={{0,4},{4,0},{8,12},{12,8},{16,20},{20,16},{24,28},{28,24},{1,5},{5... | collective-permute-start | bytes 1179656 | tf_op jit(solution)/shard_map/ppermute | solution.py:289
  958.2 35.0 %collective-permute-start.25 = (bf16[6,64,512]{2,1,0:T(8,128)(2,1)}, bf16[6,64,512]{2,1,0:T(8,128)(2,1)S(1)}, u32[]{:S(2)}, u32[]{:S(2)}) collective-permute-start(bf16[6,64,512]{2,1,0:T(8,128)(2,1)} %get-tuple-element.42), channel_id=1, source_target_pairs={{0,8},{4,12},{8,0},{12,4},{16,24},{20,28},{24,16},{28,20},{1,9},{5... | collective-permute-start | bytes 1179656 | tf_op jit(solution)/shard_map/ppermute | solution.py:289
  958.5 50.8 %collective-permute-start.26 = (bf16[6,64,512]{2,1,0:T(8,128)(2,1)}, bf16[6,64,512]{2,1,0:T(8,128)(2,1)S(1)}, u32[]{:S(2)}, u32[]{:S(2)}) collective-permute-start(bf16[6,64,512]{2,1,0:T(8,128)(2,1)} %get-tuple-element.43), channel_id=1, source_target_pairs={{0,12},{4,8},{8,4},{12,0},{16,28},{20,24},{24,20},{28,16},{1,13},{... | collective-permute-start | bytes 1179656 | tf_op jit(solution)/shard_map/ppermute | solution.py:289
  959.7 49.6 %collective-permute-start.27 = (bf16[6,64,512]{2,1,0:T(8,128)(2,1)}, bf16[6,64,512]{2,1,0:T(8,128)(2,1)S(1)}, u32[]{:S(2)}, u32[]{:S(2)}) collective-permute-start(bf16[6,64,512]{2,1,0:T(8,128)(2,1)} %get-tuple-element.44), channel_id=1, source_target_pairs={{0,16},{4,20},{8,24},{12,28},{16,0},{20,4},{24,8},{28,12},{1,17},{... | collective-permute-start | bytes 1179656 | tf_op jit(solution)/shard_map/ppermute | solution.py:289
  961.8 52.4 %collective-permute-start.28 = (bf16[6,64,512]{2,1,0:T(8,128)(2,1)}, bf16[6,64,512]{2,1,0:T(8,128)(2,1)}, u32[]{:S(2)}, u32[]{:S(2)}) collective-permute-start(bf16[6,64,512]{2,1,0:T(8,128)(2,1)} %get-tuple-element.45), channel_id=1, source_target_pairs={{0,20},{4,16},{8,28},{12,24},{16,4},{20,0},{24,12},{28,8},{1,21},{... | collective-permute-start | bytes 1179656 | tf_op jit(solution)/shard_map/ppermute | solution.py:289
  975.2 75.6 %collective-permute-start.29 = (bf16[6,64,512]{2,1,0:T(8,128)(2,1)S(1)}, bf16[6,64,512]{2,1,0:T(8,128)(2,1)S(1)}, u32[]{:S(2)}, u32[]{:S(2)}) collective-permute-start(bf16[6,64,512]{2,1,0:T(8,128)(2,1)S(1)} %copy-done.18), channel_id=1, source_target_pairs={{0,24},{4,28},{8,16},{12,20},{16,8},{20,12},{24,0},{28,4},{1,25},{... | collective-permute-start | bytes 1179656 | tf_op jit(solution)/shard_map/ppermute | solution.py:289
  993.2 70.9 %collective-permute-start.30 = (bf16[6,64,512]{2,1,0:T(8,128)(2,1)S(1)}, bf16[6,64,512]{2,1,0:T(8,128)(2,1)S(1)}, u32[]{:S(2)}, u32[]{:S(2)}) collective-permute-start(bf16[6,64,512]{2,1,0:T(8,128)(2,1)S(1)} %copy-done.16), channel_id=1, source_target_pairs={{0,28},{4,24},{8,20},{12,16},{16,12},{20,8},{24,4},{28,0},{1,29},{... | collective-permute-start | bytes 1179656 | tf_op jit(solution)/shard_map/ppermute | solution.py:289
  1223.0 7.6 collective-permute-start.38
  1225.4 51.0 %collective-permute-start.39 = (bf16[2,64,512]{2,1,0:T(8,128)(2,1)}, bf16[2,64,512]{2,1,0:T(8,128)(2,1)}, u32[]{:S(2)}, u32[]{:S(2)}) collective-permute-start(bf16[2,64,512]{2,1,0:T(8,128)(2,1)} %get-tuple-element.63), channel_id=1, source_target_pairs={{0,8},{4,12},{8,0},{12,4},{16,24},{20,28},{24,16},{28,20},{1,9},{5... | collective-permute-start | bytes 393224 | tf_op jit(solution)/shard_map/ppermute | solution.py:289
  1225.7 52.4 %collective-permute-start.40 = (bf16[2,64,512]{2,1,0:T(8,128)(2,1)}, bf16[2,64,512]{2,1,0:T(8,128)(2,1)}, u32[]{:S(2)}, u32[]{:S(2)}) collective-permute-start(bf16[2,64,512]{2,1,0:T(8,128)(2,1)} %get-tuple-element.64), channel_id=1, source_target_pairs={{0,12},{4,8},{8,4},{12,0},{16,28},{20,24},{24,20},{28,16},{1,13},{... | collective-permute-start | bytes 393224 | tf_op jit(solution)/shard_map/ppermute | solution.py:289
  1226.9 52.1 %collective-permute-start.41 = (bf16[2,64,512]{2,1,0:T(8,128)(2,1)}, bf16[2,64,512]{2,1,0:T(8,128)(2,1)}, u32[]{:S(2)}, u32[]{:S(2)}) collective-permute-start(bf16[2,64,512]{2,1,0:T(8,128)(2,1)} %get-tuple-element.65), channel_id=1, source_target_pairs={{0,16},{4,20},{8,24},{12,28},{16,0},{20,4},{24,8},{28,12},{1,17},{... | collective-permute-start | bytes 393224 | tf_op jit(solution)/shard_map/ppermute | solution.py:289
  1229.4 71.1 %collective-permute-start.31 = (bf16[4,64,512]{2,1,0:T(8,128)(2,1)}, bf16[4,64,512]{2,1,0:T(8,128)(2,1)}, u32[]{:S(2)}, u32[]{:S(2)}) collective-permute-start(bf16[4,64,512]{2,1,0:T(8,128)(2,1)} %get-tuple-element.49), channel_id=1, source_target_pairs={{0,4},{4,0},{8,12},{12,8},{16,20},{20,16},{24,28},{28,24},{1,5},{5... | collective-permute-start | bytes 786440 | tf_op jit(solution)/shard_map/ppermute | solution.py:289
  1231.2 69.2 %collective-permute-start.32 = (bf16[4,64,512]{2,1,0:T(8,128)(2,1)}, bf16[4,64,512]{2,1,0:T(8,128)(2,1)}, u32[]{:S(2)}, u32[]{:S(2)}) collective-permute-start(bf16[4,64,512]{2,1,0:T(8,128)(2,1)} %get-tuple-element.50), channel_id=1, source_target_pairs={{0,8},{4,12},{8,0},{12,4},{16,24},{20,28},{24,16},{28,20},{1,9},{5... | collective-permute-start | bytes 786440 | tf_op jit(solution)/shard_map/ppermute | solution.py:289
  1276.5 13.0 collective-permute-start.42
  1278.2 16.2 %collective-permute-start.43 = (bf16[2,64,512]{2,1,0:T(8,128)(2,1)}, bf16[2,64,512]{2,1,0:T(8,128)(2,1)S(1)}, u32[]{:S(2)}, u32[]{:S(2)}) collective-permute-start(bf16[2,64,512]{2,1,0:T(8,128)(2,1)} %copy-done.25), channel_id=1, source_target_pairs={{0,24},{4,28},{8,16},{12,20},{16,8},{20,12},{24,0},{28,4},{1,25},{... | collective-permute-start | bytes 393224 | tf_op jit(solution)/shard_map/ppermute | solution.py:289
  1279.0 21.4 %collective-permute-start.44 = (bf16[2,64,512]{2,1,0:T(8,128)(2,1)}, bf16[2,64,512]{2,1,0:T(8,128)(2,1)S(1)}, u32[]{:S(2)}, u32[]{:S(2)}) collective-permute-start(bf16[2,64,512]{2,1,0:T(8,128)(2,1)} %copy-done.24), channel_id=1, source_target_pairs={{0,28},{4,24},{8,20},{12,16},{16,12},{20,8},{24,4},{28,0},{1,29},{... | collective-permute-start | bytes 393224 | tf_op jit(solution)/shard_map/ppermute | solution.py:289
  1289.4 17.7 %collective-permute-start.33 = (bf16[4,64,512]{2,1,0:T(8,128)(2,1)}, bf16[4,64,512]{2,1,0:T(8,128)(2,1)S(1)}, u32[]{:S(2)}, u32[]{:S(2)}) collective-permute-start(bf16[4,64,512]{2,1,0:T(8,128)(2,1)} %copy-done.23), channel_id=1, source_target_pairs={{0,12},{4,8},{8,4},{12,0},{16,28},{20,24},{24,20},{28,16},{1,13},{... | collective-permute-start | bytes 786440 | tf_op jit(solution)/shard_map/ppermute | solution.py:289
  1294.3 12.8 collective-permute-start.34
  1300.4 29.2 %collective-permute-start.35 = (bf16[4,64,512]{2,1,0:T(8,128)(2,1)}, bf16[4,64,512]{2,1,0:T(8,128)(2,1)S(1)}, u32[]{:S(2)}, u32[]{:S(2)}) collective-permute-start(bf16[4,64,512]{2,1,0:T(8,128)(2,1)} %copy-done.21), channel_id=1, source_target_pairs={{0,20},{4,16},{8,28},{12,24},{16,4},{20,0},{24,12},{28,8},{1,21},{... | collective-permute-start | bytes 786440 | tf_op jit(solution)/shard_map/ppermute | solution.py:289
  1300.4 37.2 %collective-permute-start.36 = (bf16[4,64,512]{2,1,0:T(8,128)(2,1)}, bf16[4,64,512]{2,1,0:T(8,128)(2,1)S(1)}, u32[]{:S(2)}, u32[]{:S(2)}) collective-permute-start(bf16[4,64,512]{2,1,0:T(8,128)(2,1)} %copy-done.20), channel_id=1, source_target_pairs={{0,24},{4,28},{8,16},{12,20},{16,8},{20,12},{24,0},{28,4},{1,25},{... | collective-permute-start | bytes 786440 | tf_op jit(solution)/shard_map/ppermute | solution.py:289
  1300.4 44.2 %collective-permute-start.37 = (bf16[4,64,512]{2,1,0:T(8,128)(2,1)}, bf16[4,64,512]{2,1,0:T(8,128)(2,1)S(1)}, u32[]{:S(2)}, u32[]{:S(2)}) collective-permute-start(bf16[4,64,512]{2,1,0:T(8,128)(2,1)} %copy-done.19), channel_id=1, source_target_pairs={{0,28},{4,24},{8,20},{12,16},{16,12},{20,8},{24,4},{28,0},{1,29},{... | collective-permute-start | bytes 786440 | tf_op jit(solution)/shard_map/ppermute | solution.py:289
  (178 other events, 2977.2 us)
Sparse Core Ops, SparseCore 0:
  11.4 97.6 all-gather.3
  842.1 105.6 reduce-scatter.2
  952.3 154.6 reduce-scatter.4

commit v2 on v1

v2 whole, which is shorter than its diff:
```python
import functools
import math

import jax
import jax.numpy as jnp
from jax import lax
from jax.experimental import pallas as pl
from jax.experimental.pallas import tpu as pltpu
from jax.sharding import PartitionSpec as P

HEADS = 8
FF = 2048
BLOCK = 16
LAYERS = 2
STEP = 10
MAX_LEN = 4096


HIGH = lax.Precision.HIGHEST
LN_TWO = math.log(2.0)
NEG_FILL = -1e30
NORM_EPS = 1e-05
ADAM_EPS = 1e-08
RATE_MATRIX = 0.03
RATE_VECTOR = 0.2
WEIGHT_DECAY = 0.01
BETA_ONE = 0.9
BETA_TWO = 0.95
BETA_STAT = 0.95

PANEL = 8
LANES = 128
UNIT_COUNT = 24
UNIT_OPT = 0
UNIT_ROW = UNIT_COUNT
UNIT_SLOT = 2 * UNIT_COUNT
DIAG = 128
VMEM_GRANT = 48 * 2**20
IN_VMEM = pl.BlockSpec(memory_space=pltpu.VMEM)
IN_SMEM = pl.BlockSpec(memory_space=pltpu.SMEM)
ANYWHERE = pl.BlockSpec(memory_space=pl.ANY)


def contract(left, right, left_dim, right_dim, precision=None):
    return lax.dot_general(
        left,
        right,
        (((left_dim,), (right_dim,)), ((), ())),
        precision=precision,
        preferred_element_type=jnp.float32,
    )


def split_two(values):
    high = values.astype(jnp.bfloat16)
    return (high, (values - high.astype(jnp.float32)).astype(jnp.bfloat16))


def wide_left(left, right_low, left_dim, right_dim):
    high, rest = split_two(left)
    return contract(high, right_low, left_dim, right_dim) + contract(
        rest, right_low, left_dim, right_dim
    )


def wide_right(left_low, right, left_dim, right_dim):
    high, rest = split_two(right)
    return contract(left_low, high, left_dim, right_dim) + contract(
        left_low, rest, left_dim, right_dim
    )


def call_kernel(
    body, out_shapes, scratch, name, *operands, smem_count=0, any_in=(), any_out=(), aliases=None
):
    def place(at, listed):
        return ANYWHERE if at in listed else IN_VMEM

    return pl.pallas_call(
        body,
        out_shape=out_shapes,
        in_specs=[
            IN_SMEM if at < smem_count else place(at, any_in) for at in range(len(operands))
        ],
        out_specs=[place(at, any_out) for at in range(len(out_shapes))],
        scratch_shapes=scratch,
        input_output_aliases=aliases or {},
        compiler_params=pltpu.CompilerParams(vmem_limit_bytes=VMEM_GRANT),
        name=name,
    )(*operands)


def eliminate(left_part, right_part, turn):
    width = left_part.shape[1]
    turned = pltpu.roll(left_part, turn, 1)
    row_at = lax.broadcasted_iota(jnp.int32, (PANEL, width), 0)
    columns = [
        jnp.broadcast_to(turned[:, i : i + 1], (PANEL, width)) for i in range(PANEL)
    ]
    pivots = jnp.ones((PANEL, width), jnp.float32)
    for i in range(PANEL):
        pivot = jnp.broadcast_to(columns[i][i : i + 1, :], (PANEL, width))
        factor = jnp.where(row_at > i, columns[i] * pltpu.reciprocal(pivot, approx=False), 0.0)
        pivots = jnp.where(row_at == i, pivot, pivots)
        left_part = left_part - factor * jnp.broadcast_to(left_part[i : i + 1, :], (PANEL, width))
        right_part = right_part - factor * jnp.broadcast_to(
            right_part[i : i + 1, :], (PANEL, width)
        )
        for j in range(i + 1, PANEL):
            columns[j] = columns[j] - factor * jnp.broadcast_to(
                columns[j][i : i + 1, :], (PANEL, width)
            )
    scale = lax.rsqrt(pivots)
    return (left_part * scale, right_part * scale)


def factorize(gram, upper, work, inverses):
    count, size, _ = gram.shape
    blocks = size // DIAG
    eye = (
        lax.broadcasted_iota(jnp.int32, (DIAG, DIAG), 0)
        == lax.broadcasted_iota(jnp.int32, (DIAG, DIAG), 1)
    ).astype(jnp.float32)
    for block_at in range(blocks):
        low, top = (block_at * DIAG, (block_at + 1) * DIAG)
        for m in range(count):
            work[m, :, 0:DIAG] = gram[m, low:top, low:top]
            work[m, :, DIAG:] = eye

        def panel(panel_at, carry):
            row = pl.multiple_of(panel_at * PANEL, PANEL)
            turn = lax.rem(DIAG - panel_at * PANEL, DIAG)
            for m in range(count):
                left_part, right_part = eliminate(
                    work[m, pl.ds(row, PANEL), 0:DIAG], work[m, pl.ds(row, PANEL), DIAG:], turn
                )
                inverses[m, block_at, pl.ds(row, PANEL), :] = right_part
                both = jnp.concatenate([left_part, right_part], axis=1)
                work[m] = work[m] - contract(left_part, both, 0, 0, HIGH)
            return carry

        lax.fori_loop(0, DIAG // PANEL, panel, 0)
        for m in range(count):
            if block_at + 1 < blocks:
                right_of = contract(inverses[m, block_at], gram[m, low:top, top:], 1, 0, HIGH)
                upper[m, low:top, top:] = right_of
                for other in range(block_at + 1, blocks):
                    skip = (other - block_at - 1) * DIAG
                    gram[m, other * DIAG : (other + 1) * DIAG, other * DIAG :] -= contract(
                        right_of[:, skip : skip + DIAG], right_of[:, skip:], 0, 0, HIGH
                    )


def renew_body(piece_count, *refs):
    offset_ref, stat_ref, basis_ref = refs[:3]
    piece_refs = refs[3 : 3 + piece_count]
    product, gram, upper, work, inverses = refs[3 + piece_count :]
    count, size, _ = stat_ref.shape
    for m in range(count):
        product[m] = wide_left(stat_ref[m], basis_ref[m], 1, 0)
        gram[m] = contract(product[m], product[m], 0, 0, HIGH)
    factorize(gram, upper, work, inverses)
    for low in range(0, size, DIAG):
        top = low + DIAG
        for m in range(count):
            rest = product[m, :, low:top]
            if low:
                rest = rest - contract(product[m, :, :low], upper[m, :low, low:top], 1, 0, HIGH)
            product[m, :, low:top] = contract(rest, inverses[m, low // DIAG], 1, 1, HIGH)
    rows = piece_refs[0].shape[1]
    for piece_at in range(piece_count):
        row = pl.multiple_of(offset_ref[piece_at], 8)
        piece_refs[piece_at][...] = product[:, pl.ds(row, rows), :].astype(jnp.bfloat16)


def renew_bases(offsets, new_stat, basis_low):
    count, size, _ = new_stat.shape
    piece_count = offsets.shape[0]
    square = pltpu.VMEM((count, size, size), jnp.float32)
    return call_kernel(
        functools.partial(renew_body, piece_count),
        [
            jax.ShapeDtypeStruct((count, size // piece_count, size), jnp.bfloat16)
            for _ in range(piece_count)
        ],
        [
            square,
            square,
            square,
            pltpu.VMEM((count, DIAG, 2 * DIAG), jnp.float32),
            pltpu.VMEM((count, size // DIAG, DIAG, DIAG), jnp.float32),
        ],
        "renew_bases",
        offsets,
        new_stat,
        basis_low,
        smem_count=1,
    )


def pack_body(slot_ref, stats, bases, first, second, *piece_refs):
    for piece_at, piece_ref in enumerate(piece_refs):
        slot = slot_ref[piece_at]
        piece_ref[0:2] = stats[slot].astype(jnp.bfloat16)
        piece_ref[2:4] = bases[slot].astype(jnp.bfloat16)
        piece_ref[4] = first[slot].astype(jnp.bfloat16)
        piece_ref[5] = second[slot].astype(jnp.bfloat16)


def rotate_body(piece_count, *refs):
    offset_ref, grad_ref = refs[:2]
    given = refs[2 : 2 + piece_count]
    sent = refs[2 + piece_count : 2 + 2 * piece_count]
    stat_ref, basis_ref, whole, results = refs[2 + 2 * piece_count :]
    rows = given[0].shape[1]
    for piece_at in range(piece_count):
        row = pl.multiple_of(offset_ref[piece_at], 8)
        whole[:, pl.ds(row, rows), :] = given[piece_at][...].astype(jnp.float32)
    grad = grad_ref[...]
    left = whole[2].astype(jnp.bfloat16)
    right = whole[3].astype(jnp.bfloat16)
    basis_ref[0] = left
    basis_ref[1] = right
    results[0] = contract(grad, grad, 1, 1)
    results[1] = contract(grad, grad, 0, 0)
    stat_ref[0] = BETA_STAT * whole[0] + (1.0 - BETA_STAT) * results[0]
    stat_ref[1] = BETA_STAT * whole[1] + (1.0 - BETA_STAT) * results[1]
    rotated = wide_left(contract(left, grad, 0, 0), right, 1, 0)
    results[2] = rotated
    new_first = BETA_ONE * whole[4] + (1.0 - BETA_ONE) * rotated
    new_second = BETA_TWO * whole[5] + (1.0 - BETA_TWO) * rotated * rotated
    direction = (
        new_first
        / (1.0 - BETA_ONE**STEP)
        / (jnp.sqrt(new_second / (1.0 - BETA_TWO**STEP)) + ADAM_EPS)
    )
    results[3] = wide_right(left, wide_left(direction, right, 1, 1), 1, 0)
    for piece_at in range(piece_count):
        row = pl.multiple_of(offset_ref[piece_at], 8)
        sent[piece_at][...] = results[:, pl.ds(row, rows), :].astype(jnp.bfloat16)


def rotate_slot(offsets, grad, pieces):
    size = grad.shape[0]
    piece_count = offsets.shape[0]
    return call_kernel(
        functools.partial(rotate_body, piece_count),
        [
            jax.ShapeDtypeStruct((4, size // piece_count, size), jnp.bfloat16)
            for _ in range(piece_count)
        ]
        + [
            jax.ShapeDtypeStruct((2, size, size), jnp.float32),
            jax.ShapeDtypeStruct((2, size, size), jnp.bfloat16),
        ],
        [
            pltpu.VMEM((6, size, size), jnp.float32),
            pltpu.VMEM((4, size, size), jnp.float32),
        ],
        "rotate_slot",
        offsets,
        grad,
        *pieces,
        smem_count=1,
    )


def finish_body(own_slots, piece_count, *refs):
    slot_ref, masters, first, second, stats = refs[:5]
    given = refs[5 : 5 + piece_count]
    new_masters, new_first, new_second, new_stats = refs[5 + piece_count :]
    for piece_at in range(piece_count):
        slot = slot_ref[piece_at]

        @pl.when(slot < own_slots)
        def _():
            piece = given[piece_at]
            rotated = piece[2].astype(jnp.float32)
            update = piece[3].astype(jnp.float32)
            new_first[slot] = BETA_ONE * first[slot] + (1.0 - BETA_ONE) * rotated
            new_second[slot] = BETA_TWO * second[slot] + (1.0 - BETA_TWO) * rotated * rotated
            new_masters[slot] = masters[slot] - RATE_MATRIX * (
                update + WEIGHT_DECAY * masters[slot]
            )
            new_stats[slot] = BETA_STAT * stats[slot] + (1.0 - BETA_STAT) * piece[
                0:2
            ].astype(jnp.float32)


def place_body(own_slots, slot_ref, *refs):
    new_bases = refs[-1]
    for piece_at, piece in enumerate(refs[:-1]):
        slot = slot_ref[piece_at]

        @pl.when(slot < own_slots)
        def _():
            new_bases[slot] = piece[...].astype(jnp.float32)


def swap_pieces(pieces, axis):
    device_count = lax.axis_size(axis)
    return [pieces[0]] + [
        lax.ppermute(pieces[k], axis, [(i, i ^ k) for i in range(device_count)])
        for k in range(1, device_count)
    ]


def to_owners(pieces, axis, by_permutes):
    if by_permutes:
        return swap_pieces(pieces, axis)
    stacked = jnp.stack(pieces)
    device_count = lax.axis_size(axis)
    padded = jnp.pad(stacked, [(0, device_count - len(pieces))] + [(0, 0)] * (stacked.ndim - 1))
    swapped = lax.all_to_all(padded, axis, 0, 0, tiled=True)
    kinds, _, width = pieces[0].shape
    return [jnp.swapaxes(swapped, 0, 1).reshape(kinds, -1, width)]


def to_homes(pieces, axis, by_permutes, own_slots):
    if by_permutes:
        return swap_pieces(pieces, axis)
    kinds, _, width = pieces[0].shape
    device_count = lax.axis_size(axis)
    shaped = jnp.swapaxes(pieces[0].reshape(kinds, device_count, -1, width), 0, 1)
    swapped = lax.all_to_all(shaped, axis, 0, 0, tiled=True)
    return [swapped[slot] for slot in range(own_slots)]


def partner(value, axis, apart):
    return lax.ppermute(value, axis, [(i, i ^ 1 << apart) for i in range(lax.axis_size(axis))])


def pair_mean(values):
    shaped = values.reshape((values.shape[0] // 2, 2) + values.shape[1:])
    return 0.5 * (shaped[:, 0] + shaped[:, 1])


def pair_spread(grads):
    return 0.5 * jnp.repeat(grads, 2, axis=0)


def sum_rows(values):
    return jnp.sum(values, axis=0, keepdims=True)


def norm_parts(values):
    centred = values - jnp.mean(values, axis=-1, keepdims=True)
    recip = lax.rsqrt(jnp.mean(centred * centred, axis=-1, keepdims=True) + NORM_EPS)
    return (centred * recip, recip)


def norm_back(grad, gain, normed, recip):
    scaled = grad * gain
    return recip * (
        scaled
        - jnp.mean(scaled, axis=-1, keepdims=True)
        - normed * jnp.mean(scaled * normed, axis=-1, keepdims=True)
    )


def half_matrix(shape, fine_dim):
    fine = lax.broadcasted_iota(jnp.int32, shape, fine_dim)
    coarse = lax.broadcasted_iota(jnp.int32, shape, 1 - fine_dim)
    return jnp.where(fine >> 1 == coarse, 0.5, 0.0).astype(jnp.bfloat16)


def pool(rows_low):
    count = rows_low.shape[0]
    return contract(half_matrix((count // 2, count), 1), rows_low, 1, 0).astype(jnp.bfloat16)


def spread(grads):
    count = grads.shape[0]
    return wide_right(half_matrix((2 * count, count), 0), grads, 1, 0)


def norm_cdf(values):
    return 0.5 * (1.0 + lax.erf(values * math.sqrt(0.5)))


def local_count(tok_count):
    return (tok_count // BLOCK).bit_length() - 1


def key_width(tok_count, tree_bits):
    rows = 2 * (tok_count - BLOCK) + BLOCK * tree_bits
    return -(-rows // LANES) * LANES


def score_offsets(tok_count, tree_bits, span_bits):
    token = jnp.arange(tok_count, dtype=jnp.int32)[:, None]
    parts = []
    for height in range(local_count(tok_count)):
        row = jnp.arange(tok_count >> height, dtype=jnp.int32)[None, :]
        apart = token // (BLOCK << height) ^ row // BLOCK
        counted = apart <= 1 if height == 0 else apart == 1
        parts.append(jnp.where(counted, height * LN_TWO, NEG_FILL))
    for bit_at in range(tree_bits):
        offset = (local_count(tok_count) + bit_at) * LN_TWO
        parts.append(
            jnp.broadcast_to(
                jnp.where(bit_at + 1 <= span_bits, offset, NEG_FILL), (tok_count, BLOCK)
            )
        )
    used = sum(part.shape[1] for part in parts)
    rest = key_width(tok_count, tree_bits) - used
    parts.append(jnp.full((tok_count, rest), NEG_FILL, jnp.float32))
    return jnp.concatenate(parts, axis=1).astype(jnp.float32)


def stack_keys(own_rows, far_rows):
    parts = [own_rows]
    for _ in range(local_count(own_rows.shape[0]) - 1):
        parts.append(pool(parts[-1]))
    parts = parts + far_rows
    rest = key_width(own_rows.shape[0], len(far_rows)) - sum(part.shape[0] for part in parts)
    if rest:
        parts.append(jnp.zeros((rest, own_rows.shape[1]), jnp.bfloat16))
    return jnp.concatenate(parts, axis=0)


def by_heads(pair):
    lane = lax.broadcasted_iota(jnp.int32, pair.shape, 1)
    zero = jnp.zeros_like(pair)
    first = lane < LANES // 2
    return jnp.concatenate([jnp.where(first, pair, zero), jnp.where(first, zero, pair)], axis=0)


def from_heads(both):
    count = both.shape[0] // 2
    lane = lax.broadcasted_iota(jnp.int32, (count, LANES), 1)
    return jnp.where(lane < LANES // 2, both[:count], both[count:])


def attend(qkv, far_rows, offsets, probs, mixed):
    width = qkv.shape[1] // 3
    score_scale = (width // HEADS) ** (-0.5)
    stack = stack_keys(qkv[:, width:], far_rows)
    both_offsets = jnp.concatenate([offsets, offsets], axis=0)
    for pair_at in range(width // LANES):
        low, top = (pair_at * LANES, (pair_at + 1) * LANES)
        scores = (
            contract(by_heads(qkv[:, low:top]), stack[:, low:top], 1, 1) * score_scale
            + both_offsets
        )
        expo = jnp.exp(scores - jnp.max(scores, axis=1, keepdims=True))
        weights = expo / jnp.sum(expo, axis=1, keepdims=True)
        probs[pair_at] = weights
        result = contract(
            weights.astype(jnp.bfloat16), stack[:, width + low : width + top], 1, 0
        )
        mixed[:, low:top] = from_heads(result).astype(jnp.bfloat16)


def attend_back(qkv, far_rows, probs, mixed_grad, query_grad, key_grads, far_grads):
    tok_count, width = mixed_grad.shape
    score_scale = (width // HEADS) ** (-0.5)
    stack = stack_keys(qkv[:, width:], far_rows)
    local_levels = local_count(tok_count)
    far_start = 2 * (tok_count - BLOCK)
    for pair_at in range(width // LANES):
        low, top = (pair_at * LANES, (pair_at + 1) * LANES)
        queries = by_heads(qkv[:, low:top])
        grads = by_heads(mixed_grad[:, low:top])
        weights = probs[pair_at]
        prob_grad = contract(grads, stack[:, width + low : width + top], 1, 1)
        inner = jnp.sum(weights * prob_grad, axis=1, keepdims=True)
        score_grad = (weights * (prob_grad - inner)).astype(jnp.bfloat16)
        query_grad[:, low:top] = (
            from_heads(contract(score_grad, stack[:, low:top], 1, 0)) * score_scale
        ).astype(jnp.bfloat16)
        for start, part in (
            (low, contract(score_grad, queries, 0, 0) * score_scale),
            (width + low, contract(weights.astype(jnp.bfloat16), grads, 0, 0)),
        ):
            for far_at, far_grad in enumerate(far_grads):
                row = far_start + BLOCK * far_at
                far_grad[:, start : start + LANES] = part[row : row + BLOCK]
            folded = None
            for height in reversed(range(local_levels)):
                row = 2 * (tok_count - (tok_count >> height))
                own = part[row : row + (tok_count >> height)]
                folded = own if folded is None else own + spread(folded)
            key_grads[:, start : start + LANES] = folded


class Units:
    def __init__(self, meta, packed, store, sems, units):
        self.store = store
        self.place = {unit: at for at, unit in enumerate(units)}
        self.waiting = {}
        rows = store.shape[2]
        for at, unit in enumerate(units):
            row = pl.multiple_of(meta[UNIT_ROW + unit], rows)
            copy = pltpu.make_async_copy(
                packed.at[:, meta[UNIT_OPT + unit], pl.ds(row, rows), :],
                store.at[at],
                sems.at[at],
            )
            copy.start()
            self.waiting[unit] = copy

    def __getitem__(self, unit):
        if unit in self.waiting:
            self.waiting.pop(unit).wait()
        width = self.store.shape[3]
        return self.store[self.place[unit]].reshape(width, width)


class Grads:
    def __init__(self, meta, slots, store, sems):
        self.meta, self.slots, self.store, self.sems = (meta, slots, store, sems)
        self.copies = []

    def put(self, unit, left_low, right_low):
        at = len(self.copies)
        self.store[at] = contract(left_low, right_low, 0, 0).astype(jnp.bfloat16)
        copy = pltpu.make_async_copy(
            self.store.at[at], self.slots.at[self.meta[UNIT_SLOT + unit]], self.sems.at[at]
        )
        copy.start()
        self.copies.append(copy)

    def finish(self):
        for copy in self.copies:
            copy.wait()


def project(hidden, units, first_unit, gain, bias, normed_ref, qkv_ref, near_ref):
    width = hidden.shape[1]
    normed, _ = norm_parts(hidden)
    normed_low = (normed * gain + bias).astype(jnp.bfloat16)
    normed_ref[...] = normed_low
    for part in range(3):
        qkv_ref[:, part * width : (part + 1) * width] = contract(
            normed_low, units[first_unit + part], 1, 0
        ).astype(jnp.bfloat16)
    near = qkv_ref[:, width:]
    for _ in range(local_count(near.shape[0])):
        near = pool(near)
    near_ref[...] = near


def feed_forward(middle, units, first_unit, vec, vec_at, normed_ref, pre_ref, act_ref):
    width = middle.shape[1]
    normed, _ = norm_parts(middle)
    normed_low = (normed * vec[vec_at + 2 : vec_at + 3] + vec[vec_at + 3 : vec_at + 4]).astype(
        jnp.bfloat16
    )
    normed_ref[...] = normed_low
    total = middle
    ff_blocks = FF // width
    for part in range(ff_blocks):
        low, top = (part * width, (part + 1) * width)
        row = vec_at + 4 + part
        pre = contract(normed_low, units[first_unit + 4 + part], 1, 0) + vec[row : row + 1]
        act = (pre * norm_cdf(pre)).astype(jnp.bfloat16)
        pre_ref[:, low:top] = pre
        act_ref[:, low:top] = act
        total = total + contract(act, units[first_unit + 4 + ff_blocks + part], 1, 0)
    row = vec_at + 4 + ff_blocks
    return total + vec[row : row + 1]


def feed_back(
    grad, middle, normed_low, pre_ref, act_ref, units, grads, first_unit, vec, vec_at, vec_grads, at
):
    width = middle.shape[1]
    ff_blocks = FF // width
    down_grad = grad.astype(jnp.bfloat16)
    normed_grad = jnp.zeros(middle.shape, jnp.float32)
    for part in range(ff_blocks):
        low, top = (part * width, (part + 1) * width)
        down_unit = first_unit + 4 + ff_blocks + part
        grads.put(down_unit, act_ref[:, low:top], down_grad)
        pre = pre_ref[:, low:top]
        slope = norm_cdf(pre) + pre * jnp.exp(-0.5 * pre * pre) * (1.0 / math.sqrt(2.0 * math.pi))
        pre_grad = (contract(down_grad, units[down_unit], 1, 1) * slope).astype(jnp.bfloat16)
        grads.put(first_unit + 4 + part, normed_low, pre_grad)
        vec_grads[at + 2 + part : at + 3 + part] = sum_rows(pre_grad.astype(jnp.float32))
        normed_grad = normed_grad + contract(pre_grad, units[first_unit + 4 + part], 1, 1)
    row = at + 2 + ff_blocks
    vec_grads[row : row + 1] = sum_rows(grad)
    normed, recip = norm_parts(middle)
    vec_grads[at : at + 1] = sum_rows(normed_grad * normed)
    vec_grads[at + 1 : at + 2] = sum_rows(normed_grad)
    return grad + norm_back(normed_grad, vec[vec_at + 2 : vec_at + 3], normed, recip)


def project_back(
    middle_grad, hidden, normed_low, query_grad, key_grads, near_grads, units, grads, first_unit,
    vec, vec_at, vec_grads,
):
    width = hidden.shape[1]
    near = near_grads[...]
    for _ in range(local_count(hidden.shape[0])):
        near = spread(near)
    rows_low = (key_grads[...] + near).astype(jnp.bfloat16)
    parts = (query_grad[...], rows_low[:, :width], rows_low[:, width:])
    normed_grad = jnp.zeros(hidden.shape, jnp.float32)
    for part, part_grad in enumerate(parts):
        grads.put(first_unit + part, normed_low, part_grad)
        normed_grad = normed_grad + contract(part_grad, units[first_unit + part], 1, 1)
    normed, recip = norm_parts(hidden)
    vec_grads[0:1] = sum_rows(normed_grad * normed)
    vec_grads[1:2] = sum_rows(normed_grad)
    return middle_grad + norm_back(normed_grad, vec[vec_at : vec_at + 1], normed, recip)


def first_body(per_layer, meta, vec, inputs, packed, normed, qkv, near, store, sems):
    units = Units(meta, packed, store, sems, range(3))
    project(inputs[...].astype(jnp.float32), units, 0, vec[0:1], vec[1:2], normed, qkv, near)


def middle_body(per_layer, vec_rows, tree_bits, meta, vec, offsets, inputs, qkv, *refs):
    far, refs = (refs[:tree_bits], refs[tree_bits:])
    packed, probs, mixed, middle, normed_two, pre, act, hidden, normed, next_qkv, near = refs[:11]
    store, sems = refs[11:]
    units = Units(meta, packed, store, sems, range(3, per_layer + 3))
    attend(qkv[...], [ref[...] for ref in far], offsets[...], probs, mixed)
    middle[...] = inputs[...].astype(jnp.float32) + contract(mixed[...], units[3], 1, 0)
    hidden[...] = feed_forward(middle[...], units, 0, vec, 0, normed_two, pre, act)
    project(
        hidden[...], units, per_layer, vec[vec_rows : vec_rows + 1],
        vec[vec_rows + 1 : vec_rows + 2], normed, next_qkv, near,
    )


def turn_body(per_layer, vec_rows, tree_bits, meta, vec, offsets, cotangent, hidden, qkv, *refs):
    far, refs = (refs[:tree_bits], refs[tree_bits:])
    packed, outputs, middle_grad, query_grad, key_grads, vec_grads, slots = refs[:7]
    far_grads, refs = (refs[7 : 7 + tree_bits], refs[7 + tree_bits :])
    store, sems, grad_store, grad_sems, probs, mixed, normed_two, pre, act = refs
    units = Units(meta, packed, store, sems, range(per_layer + 3, 2 * per_layer))
    grads = Grads(meta, slots, grad_store, grad_sems)
    far_rows = [ref[...] for ref in far]
    attend(qkv[...], far_rows, offsets[...], probs, mixed)
    middle = hidden[...] + contract(mixed[...], units[per_layer + 3], 1, 0)
    outputs[...] = feed_forward(
        middle, units, per_layer, vec, vec_rows, normed_two, pre, act
    ).astype(jnp.bfloat16)
    vec_grads[...] = jnp.zeros_like(vec_grads)
    grad = feed_back(
        cotangent[...].astype(jnp.float32), middle, normed_two[...], pre, act, units, grads,
        per_layer, vec, vec_rows, vec_grads, 2,
    )
    middle_grad[...] = grad
    branch_grad = grad.astype(jnp.bfloat16)
    grads.put(per_layer + 3, mixed[...], branch_grad)
    mixed_grad = contract(branch_grad, units[per_layer + 3], 1, 1).astype(jnp.bfloat16)
    attend_back(qkv[...], far_rows, probs, mixed_grad, query_grad, key_grads, far_grads)
    grads.finish()


def lower_body(per_layer, vec_rows, tree_bits, meta, vec, *refs):
    hidden, normed_one, query_in, key_in, near_in, middle_in = refs[:6]
    probs, mixed, middle, normed_two, pre, act, qkv = refs[6:13]
    far, refs = (refs[13 : 13 + tree_bits], refs[13 + tree_bits :])
    packed, _, middle_grad, query_grad, key_grads, vec_grads, slots = refs[:7]
    far_grads, refs = (refs[7 : 7 + tree_bits], refs[7 + tree_bits :])
    store, sems, grad_store, grad_sems = refs
    upper_units = list(range(per_layer, per_layer + 3))
    units = Units(
        meta, packed, store, sems, upper_units + list(range(3 + (per_layer - 4) // 2 + 1, per_layer))
        + list(range(3, 3 + (per_layer - 4) // 2 + 1)),
    )
    grads = Grads(meta, slots, grad_store, grad_sems)
    vec_grads[...] = jnp.zeros_like(vec_grads)
    grad = project_back(
        middle_in[...], hidden[...], normed_one[...], query_in, key_in, near_in, units, grads,
        per_layer, vec, vec_rows, vec_grads,
    )
    grad = feed_back(
        grad, middle[...], normed_two[...], pre, act, units, grads, 0, vec, 0, vec_grads, 2
    )
    middle_grad[...] = grad
    branch_grad = grad.astype(jnp.bfloat16)
    grads.put(3, mixed[...], branch_grad)
    mixed_grad = contract(branch_grad, units[3], 1, 1).astype(jnp.bfloat16)
    attend_back(
        qkv[...], [ref[...] for ref in far], probs, mixed_grad, query_grad, key_grads, far_grads
    )
    grads.finish()


def last_body(meta, vec, inputs, normed_one, query_in, key_in, near_in, middle_in, *refs):
    packed, _, input_grad, vec_grads, slots, store, sems, grad_store, grad_sems = refs
    units = Units(meta, packed, store, sems, range(3))
    grads = Grads(meta, slots, grad_store, grad_sems)
    vec_grads[...] = jnp.zeros_like(vec_grads)
    input_grad[...] = project_back(
        middle_in[...], inputs[...].astype(jnp.float32), normed_one[...], query_in, key_in,
        near_in, units, grads, 0, vec, 0, vec_grads,
    )
    grads.finish()


def coarse_up(own, seq_index, tree_bits):
    far_list = []
    for bit_at in range(tree_bits):
        far = partner(own, "seq", bit_at)
        far_list.append(far)
        if bit_at + 1 < tree_bits:
            upper = seq_index >> bit_at & 1 == 1
            joined = jnp.where(
                upper, jnp.concatenate([far, own]), jnp.concatenate([own, far])
            ).astype(jnp.float32)
            own = pair_mean(joined).astype(jnp.bfloat16)
    return far_list


def coarse_down(far_grads, seq_index):
    above = None
    for bit_at in reversed(range(len(far_grads))):
        upper = seq_index >> bit_at & 1 == 1
        sent = far_grads[bit_at]
        own = 0.0
        if above is not None:
            wide = pair_spread(above)
            own = jnp.where(upper, wide[BLOCK:], wide[:BLOCK])
            sent = sent + jnp.where(upper, wide[:BLOCK], wide[BLOCK:])
        above = own + partner(sent.astype(jnp.bfloat16), "seq", bit_at).astype(jnp.float32)
    return above


def per_device(
    inputs,
    cotangent,
    seq_lengths,
    unit_slot,
    masters,
    first_moment,
    second_moment,
    bases,
    stats,
    vec_master,
    vec_first,
    vec_second,
):
    seq_count = lax.axis_size("seq")
    opt_count = lax.axis_size("opt")
    seq_index = lax.axis_index("seq")
    tok_count = inputs.shape[1]
    model_width = inputs.shape[2]
    own_slots = masters.shape[0]
    row_count = masters.shape[1]
    ff_blocks = FF // model_width
    per_layer = 4 + 2 * ff_blocks
    vec_width = 5 * model_width + FF
    long_devs = min(max(MAX_LEN // tok_count, 1), seq_count)
    tree_bits = long_devs.bit_length() - 1
    size = seq_count * row_count
    by_permutes = seq_count <= 8
    if by_permutes:
        relative = jnp.arange(seq_count, dtype=jnp.int32) ^ seq_index
        offsets = relative * row_count
        slot_at = relative
    else:
        offsets = jnp.zeros((1,), jnp.int32)
        slot_at = jnp.arange(own_slots, dtype=jnp.int32)
    packed_pieces = call_kernel(
        pack_body,
        [
            jax.ShapeDtypeStruct((6, row_count, model_width), jnp.bfloat16)
            for _ in range(slot_at.shape[0])
        ],
        [],
        "pack_slots",
        jnp.minimum(slot_at, own_slots - 1),
        stats,
        bases,
        first_moment,
        second_moment,
        smem_count=1,
    )
    owner_pieces = to_owners(packed_pieces, "seq", by_permutes)
    vec_count = vec_master.shape[0]
    own_rows = own_slots * row_count
    vec_block = jnp.pad(
        vec_master.astype(jnp.bfloat16)[None], [(0, 15), (0, model_width - vec_count)]
    )
    gathered = lax.all_gather(
        jnp.concatenate(
            [masters.astype(jnp.bfloat16).reshape(own_rows, model_width), vec_block]
        )[None],
        ("seq", "opt"),
        axis=0,
        tiled=True,
    )
    vec = gathered[:, own_rows, :vec_count].reshape(-1, model_width).astype(jnp.float32)
    if row_count % 16 == 0:
        unit_rows = row_count
        packed = gathered.reshape(seq_count, opt_count, own_rows + 16, model_width)
    else:
        unit_rows = size
        packed = (
            gathered[:, :own_rows]
            .reshape(seq_count, opt_count, own_slots, row_count, model_width)
            .transpose(1, 2, 0, 3, 4)
            .reshape(1, opt_count, own_slots * size, model_width)
        )
    meta = jnp.concatenate(
        [unit_slot // own_slots, unit_slot % own_slots * unit_rows, unit_slot]
    ).astype(jnp.int32)
    span_bits = jnp.zeros((), jnp.int32)
    for bit_at in range(tree_bits + 1):
        start_dev = seq_index >> bit_at << bit_at
        span_bits = jnp.where(
            seq_lengths[0, start_dev] == tok_count * (1 << bit_at), bit_at, span_bits
        )
    offsets_in = score_offsets(tok_count, tree_bits, span_bits)
    width_in = offsets_in.shape[1]
    pair_count = model_width // LANES
    vec_rows = vec_width // model_width
    square = (model_width, model_width)

    def units_in(count):
        return [
            pltpu.VMEM((count, size // unit_rows, unit_rows, model_width), jnp.bfloat16),
            pltpu.SemaphoreType.DMA((count,)),
        ]

    def grads_out(count):
        return [pltpu.VMEM((count,) + square, jnp.bfloat16), pltpu.SemaphoreType.DMA((count,))]

    def low_of(*shape):
        return jax.ShapeDtypeStruct(shape, jnp.bfloat16)

    def full_of(*shape):
        return jax.ShapeDtypeStruct(shape, jnp.float32)

    projected = [
        low_of(tok_count, model_width),
        low_of(tok_count, 3 * model_width),
        low_of(BLOCK, 2 * model_width),
    ]
    attended = [
        full_of(pair_count, 2 * tok_count, width_in),
        low_of(tok_count, model_width),
    ]
    fed = [
        low_of(tok_count, model_width),
        full_of(tok_count, FF),
        low_of(tok_count, FF),
    ]
    back = [
        full_of(tok_count, model_width),
        low_of(tok_count, model_width),
        full_of(tok_count, 2 * model_width),
        full_of(16, model_width),
        low_of(UNIT_COUNT, *square),
    ] + [full_of(BLOCK, 2 * model_width)] * tree_bits
    normed_zero, qkv_zero, near_zero = call_kernel(
        functools.partial(first_body, per_layer),
        projected,
        units_in(3),
        "project_first",
        meta,
        vec,
        inputs[0],
        packed,
        smem_count=1,
        any_in=(3,),
    )
    far_zero = coarse_up(near_zero, seq_index, tree_bits)
    (
        probs, mixed, middle, normed_two, pre, act, hidden, normed_one, qkv_one, near_one,
    ) = call_kernel(
        functools.partial(middle_body, per_layer, vec_rows, tree_bits),
        attended + [full_of(tok_count, model_width)] + fed + [full_of(tok_count, model_width)]
        + projected,
        units_in(per_layer),
        "layer_first",
        meta,
        vec,
        offsets_in,
        inputs[0],
        qkv_zero,
        *far_zero,
        packed,
        smem_count=1,
        any_in=(5 + tree_bits,),
    )
    far_one = coarse_up(near_one, seq_index, tree_bits)
    outputs, middle_grad, query_grad, key_grads, vec_grads_up, slot_grads, *far_grads = call_kernel(
        functools.partial(turn_body, per_layer, vec_rows, tree_bits),
        [low_of(tok_count, model_width)] + back,
        units_in(per_layer - 3)
        + grads_out(per_layer - 3)
        + [pltpu.VMEM(shape.shape, shape.dtype) for shape in attended + fed],
        "layer_turn",
        meta,
        vec,
        offsets_in,
        cotangent[0],
        hidden,
        qkv_one,
        *far_one,
        packed,
        smem_count=1,
        any_in=(6 + tree_bits,),
        any_out=(5,),
    )
    near_grads = coarse_down(far_grads, seq_index)
    middle_grad, query_grad, key_grads, vec_grads_mid, slot_grads, *far_grads = call_kernel(
        functools.partial(lower_body, per_layer, vec_rows, tree_bits),
        back,
        units_in(per_layer) + grads_out(per_layer),
        "layer_back",
        meta,
        vec,
        hidden,
        normed_one,
        query_grad,
        key_grads,
        near_grads,
        middle_grad,
        probs,
        mixed,
        middle,
        normed_two,
        pre,
        act,
        qkv_zero,
        *far_zero,
        packed,
        slot_grads,
        smem_count=1,
        any_in=(15 + tree_bits, 16 + tree_bits),
        any_out=(4,),
        aliases={16 + tree_bits: 4},
    )
    near_grads = coarse_down(far_grads, seq_index)
    input_grad, vec_grads_low, slot_grads = call_kernel(
        last_body,
        [full_of(tok_count, model_width), full_of(16, model_width), low_of(UNIT_COUNT, *square)],
        units_in(3) + grads_out(3),
        "project_back",
        meta,
        vec,
        inputs[0],
        normed_zero,
        query_grad,
        key_grads,
        near_grads,
        middle_grad,
        packed,
        slot_grads,
        smem_count=1,
        any_in=(8, 9),
        any_out=(2,),
        aliases={9: 2},
    )
    vec_sum = jnp.concatenate(
        [vec_grads_low[0:2], vec_grads_mid[2:vec_rows], vec_grads_mid[0:2], vec_grads_up[2:vec_rows]]
    )
    for axis in ("opt", "seq"):
        for bit_at in range(lax.axis_size(axis).bit_length() - 1):
            vec_sum = vec_sum + partner(vec_sum, axis, bit_at)
    grad_vecs = lax.dynamic_slice_in_dim(
        vec_sum.reshape(-1), (seq_index * opt_count + lax.axis_index("opt")) * vec_count, vec_count
    )
    column_grads = lax.psum_scatter(
        slot_grads, "opt", scatter_dimension=0, tiled=True
    )
    column_grads = jnp.pad(column_grads, [(0, seq_count - own_slots), (0, 0), (0, 0)])
    owner_grad = lax.psum_scatter(column_grads, "seq", scatter_dimension=0, tiled=True)[0]
    *step_pieces, owner_stat, owner_basis = rotate_slot(offsets, owner_grad, owner_pieces)
    home_pieces = to_homes(step_pieces, "seq", by_permutes, own_slots)
    base_pieces = renew_bases(offsets, owner_stat, owner_basis)
    whole_shape = jax.ShapeDtypeStruct(masters.shape, jnp.float32)
    new_masters, new_first, new_second, new_stats = call_kernel(
        functools.partial(finish_body, own_slots, len(home_pieces)),
        [whole_shape, whole_shape, whole_shape, jax.ShapeDtypeStruct(stats.shape, jnp.float32)],
        [],
        "finish_slots",
        slot_at,
        masters,
        first_moment,
        second_moment,
        stats,
        *home_pieces,
        smem_count=1,
    )
    (new_bases,) = call_kernel(
        functools.partial(place_body, own_slots),
        [jax.ShapeDtypeStruct(bases.shape, jnp.float32)],
        [],
        "place_bases",
        slot_at,
        *to_homes(base_pieces, "seq", by_permutes, own_slots),
        smem_count=1,
    )
    new_vec_first = BETA_ONE * vec_first + (1.0 - BETA_ONE) * grad_vecs
    new_vec_second = BETA_TWO * vec_second + (1.0 - BETA_TWO) * grad_vecs * grad_vecs
    new_vectors = vec_master - RATE_VECTOR * (new_vec_first / (1.0 - BETA_ONE**STEP)) / (
        jnp.sqrt(new_vec_second / (1.0 - BETA_TWO**STEP)) + ADAM_EPS
    )
    return (
        outputs[None],
        input_grad[None],
        new_masters,
        new_first,
        new_second,
        new_bases,
        new_stats,
        new_vectors,
        new_vec_first,
        new_vec_second,
    )


def solution(mesh):
    placed = (
        P("opt", "seq", None),
        P("opt", "seq", None),
        P("opt", None),
        P(),
        P("opt", "seq", None),
        P("opt", "seq", None),
        P("opt", "seq", None),
        P("opt", None, "seq", None),
        P("opt", None, "seq", None),
        P(("seq", "opt")),
        P(("seq", "opt")),
        P(("seq", "opt")),
    )
    return jax.shard_map(
        per_device,
        mesh=mesh,
        in_specs=placed,
        out_specs=(
            P("opt", "seq", None),
            P("opt", "seq", None),
            P("opt", "seq", None),
            P("opt", "seq", None),
            P("opt", "seq", None),
            P("opt", None, "seq", None),
            P("opt", None, "seq", None),
            P(("seq", "opt")),
            P(("seq", "opt")),
            P(("seq", "opt")),
        ),
        check_vma=False,
    )
```

time: 1380 us -> 705 us (0.51)
  local copies, waits for them, and re-layouts: 497 us -> 57.6 us
  matrix products: 171 us -> 0 us
  other arithmetic: 97.1 us -> 13 us
  blocking collectives: 80.8 us -> 0 us
  waiting for transfers between devices: 332 us -> 405 us
  Pallas kernels: 113 us -> 151 us
    dot_general x108 -> x0, matrix products: 171 us -> none  [the longest x28 43.3 us: seg_apply(): jnp.einsum('sqhk,skhe->sqhe', shaped, value_segs, preferred_element_type=...]
    reshape x93 -> x1, local copies, waits for them, and re-layouts: 124 us -> 1.41 us  [per_device(): vec_sum.reshape(-1)]
    unnamed x2 -> x0, blocking collectives: 80.8 us -> none
    transpose x31 -> x0, local copies, waits for them, and re-layouts: 58.1 us -> none  [the longest x10 15.7 us: seg_apply(): jnp.einsum('sqhk,skhe->sqhe', shaped, value_segs, preferred_element_type=...]
    all_gather x1, waiting for transfers between devices: 50.9 us -> 99.3 us  [per_device(): lax.all_gather(jnp.concatenate([masters.astype(jnp.bfloat16).reshape(own_...]
    convert_element_type x47 -> x16, other arithmetic: 52.1 us -> 4.76 us  [the longest x6 3.41 us: coarse_down(): sent.astype(jnp.bfloat16)]
    scatter x1 -> x0, local copies, waits for them, and re-layouts: 44.9 us -> none  [per_device(): slot_grads = jnp.zeros_like(all_units).at[unit_slot].set(all_units)]
    another operation x46 -> x0, local copies, waits for them, and re-layouts: 39.9 us -> none
  transfers between devices with their start and end apart: 48 -> 41, of which waited for: 16 -> 27; matrix products, arithmetic and copies ran while one was open for 28% -> 1% of each run, Pallas kernels for 0% -> 15%
where the time goes in v2:
time: 705 us; the launch traced here: 693 us
  waiting for transfers between devices  405 us (57%)
  Pallas kernels  151 us (21%)
  local copies, waits for them, and re-layouts  57.6 us (8%)
  starting transfers between devices  49.5 us (7%)
  between operations  17.1 us (2%)
  other arithmetic  13 us (2%)
    pallas_call x10, Pallas kernels, call_kernel(): pl.pallas_call(body, out_shape=out_shapes, in_specs=[IN_SMEM if at < smem...  151 us
    ppermute x21, waiting for transfers between devices, swap_pieces(): lax.ppermute(pieces[k], axis, [(i, i ^ k) for i in range(device_count)])  127 us
    reduce_scatter x1, waiting for transfers between devices, per_device(): lax.psum_scatter(slot_grads, 'opt', scatter_dimension=0, tiled=True)  110 us
    all_gather x1, waiting for transfers between devices, per_device(): lax.all_gather(jnp.concatenate([masters.astype(jnp.bfloat16).reshape(own_...  99.3 us
    unnamed x156, local copies, waits for them, and re-layouts  48.7 us
    reduce_scatter x1, waiting for transfers between devices, per_device(): lax.psum_scatter(column_grads, 'seq', scatter_dimension=0, tiled=True)[0]  40.5 us
    ppermute x21, starting transfers between devices, swap_pieces(): lax.ppermute(pieces[k], axis, [(i, i ^ k) for i in range(device_count)])  31.8 us
    ppermute x17, waiting for transfers between devices, partner(): lax.ppermute(value, axis, [(i, i ^ 1 << apart) for i in range(lax.axis_si...  28.7 us
  transfers between devices with their start and end apart: 41, of which 27 were waited for; matrix products, arithmetic and copies ran while one was open for 1% of the time, Pallas kernels for 15%

profile of v2, /device:TPU:11, one launch (start us, length us, event | category | flops | bytes accessed | tf_op | source)
XLA Modules:
  0.0 693.2 jit_solution(7944617113290950109)
XLA Ops:
  11.5 99.3 %all-gather.3.cloned.1.call-done = bf16[12800,512]{1,0:T(8,128)(2,1)} async-done(((bf16[400,512]{1,0:T(8,128)(2,1)}), bf16[12800,512]{1,0:T(8,128)(2,1)}) %all-gather.3.cloned.1.call-update) | async-done | bytes 13107216 | tf_op jit(solution)/shard_map/all_gather | solution.py:782
  112.8 2.7 project_first.1
  116.6 2.3 collective-permute-done.refs_0_.refs_13_
  120.2 1.8 collective-permute-done.1.refs_1_.refs_14_
  126.2 7.1 %layer_first.1 = (f32[4,256,384]{2,1,0:T(8,128)S(1)}, bf16[128,512]{1,0:T(8,128)(2,1)S(1)}, f32[128,512]{1,0:T(8,128)S(1)}, bf16[128,512]{1,0:T(8,128)(2,1)S(1)}...) custom-call(s32[72]{0:T(128)S(1)} %pad_add_fusion.meta, ...), custom_call_target="tpu_custom_call" | custom-call | tf_op jit(solution)/shard_map/layer_first/pallas_call | solution.py:79
  137.5 2.4 collective-permute-done.3.refs_0_
  144.7 2.3 collective-permute-done.5.refs_2_
  150.1 13.1 %layer_turn.1 = (bf16[128,512]{1,0:T(8,128)(2,1)}, f32[128,512]{1,0:T(8,128)S(1)}, bf16[128,512]{1,0:T(8,128)(2,1)S(1)}, f32[128,1024]{1,0:T(8,128)S(1)}, f32[16...) custom-call(s32[72]{0:T(128)S(1)} %copy-done.68, ...), custom_call_target="tpu_custom_call" | custom-call | tf_op jit(solution)/shard_map/layer_turn/pallas_call | solution.py:79
  167.3 2.3 collective-permute-done.6
  170.6 1.6 collective-permute-start.7
  175.0 2.5 collective-permute-done.8
  185.1 13.2 %layer_back.1 = (f32[128,512]{1,0:T(8,128)S(1)}, bf16[128,512]{1,0:T(8,128)(2,1)S(1)}, f32[128,1024]{1,0:T(8,128)S(1)}, f32[16,512]{1,0:T(8,128)S(1)}, bf16[24,5...) custom-call(s32[72]{0:T(128)S(1)} %copy-done.69, ...), custom_call_target="tpu_custom_call", output_to_operand_aliasing={{4}: (19, {})} | custom-call | tf_op jit(solution)/shard_map/layer_back/pallas_call | solution.py:79
  202.2 2.5 collective-permute-done.9
  205.7 1.6 collective-permute-start.10
  210.0 2.3 collective-permute-done.11
  214.4 4.7 project_back.1
  219.4 109.8 %reduce-scatter.3.cloned.1.call-done = bf16[6,512,512]{2,1,0:T(8,128)(2,1)} async-done(((bf16[24,512,512]{2,1,0:T(8,128)(2,1)}), bf16[6,512,512]{2,1,0:T(8,128)(2,1)}) %reduce-scatter.3.cloned.1.call-update) | async-done | bytes 3145744 | tf_op jit(solution)/shard_map/reduce_scatter | solution.py:963
  329.2 4.3 pad.9
  334.9 2.2 pack_slots.1
  339.9 1.6 collective-permute-start.33
  341.5 2.1 collective-permute-start.15
  343.6 6.7 collective-permute-done.12.refs_3_
  350.3 3.9 collective-permute-start.16
  354.2 14.9 %collective-permute-done.13.refs_4_ = bf16[6,64,512]{2,1,0:T(8,128)(2,1)S(1)} collective-permute-done((bf16[6,64,512]{2,1,0:T(8,128)(2,1)S(1)}, bf16[6,64,512]{2,1,0:T(8,128)(2,1)S(1)}, u32[]{:S(2)}, u32[]{:S(2)}) %collective-permute-start.13) | collective-permute-done | bytes 393248 | tf_op jit(solution)/shard_map/ppermute | solution.py:303
  369.1 4.4 collective-permute-start.17
  374.1 14.5 %collective-permute-done.14.refs_5_ = bf16[6,64,512]{2,1,0:T(8,128)(2,1)S(1)} collective-permute-done((bf16[6,64,512]{2,1,0:T(8,128)(2,1)S(1)}, bf16[6,64,512]{2,1,0:T(8,128)(2,1)S(1)}, u32[]{:S(2)}, u32[]{:S(2)}) %collective-permute-start.14) | collective-permute-done | bytes 393248 | tf_op jit(solution)/shard_map/ppermute | solution.py:303
  388.6 2.1 collective-permute-start.34
  390.7 3.2 collective-permute-done.16.refs_7_
  394.7 41.3 %collective-permute-done.17.refs_8_ = bf16[6,64,512]{2,1,0:T(8,128)(2,1)S(1)} collective-permute-done((bf16[6,64,512]{2,1,0:T(8,128)(2,1)S(1)}, bf16[6,64,512]{2,1,0:T(8,128)(2,1)S(1)}, u32[]{:S(2)}, u32[]{:S(2)}) %collective-permute-start.17) | collective-permute-done | bytes 393248 | tf_op jit(solution)/shard_map/ppermute | solution.py:303
  436.7 9.5 %collective-permute-done.18.refs_9_ = bf16[6,64,512]{2,1,0:T(8,128)(2,1)S(1)} collective-permute-done((bf16[6,64,512]{2,1,0:T(8,128)(2,1)S(1)}, bf16[6,64,512]{2,1,0:T(8,128)(2,1)S(1)}, u32[]{:S(2)}, u32[]{:S(2)}) %collective-permute-start.18) | collective-permute-done | bytes 393248 | tf_op jit(solution)/shard_map/ppermute | solution.py:303
  447.0 40.5 %reduce-scatter.5.cloned.1.call-done = bf16[1,512,512]{2,1,0:T(8,128)(2,1)} async-done(((bf16[8,512,512]{2,1,0:T(8,128)(2,1)}), bf16[1,512,512]{2,1,0:T(8,128)(2,1)}) %reduce-scatter.5.cloned.1.call-update) | async-done | bytes 524304 | tf_op jit(solution)/shard_map/reduce_scatter | solution.py:967
  491.5 5.8 rotate_slot.1
  498.0 1.6 copy-done.4
  500.8 96.4 %renew_bases.1 = (bf16[2,64,512]{2,1,0:T(8,128)(2,1)S(1)}, bf16[2,64,512]{2,1,0:T(8,128)(2,1)S(1)}, bf16[2,64,512]{2,1,0:T(8,128)(2,1)S(1)}, bf16[2,64,512]{2,1,...) custom-call(s32[8]{0:T(128)S(1)} %broadcast_multiply_fusion.refs_0_,, ...), custom_call_target="tpu_custom_call" | custom-call | tf_op jit(solution)/shard_map/renew_bases/pallas_call | solution.py:79
  599.7 3.5 collective-permute-done.35
  603.5 2.7 collective-permute-done.36
  613.4 2.4 collective-permute-start.30
  617.4 1.6 collective-permute-start.32
  619.0 6.2 collective-permute-done.30.refs_5_
  626.5 4.4 collective-permute-start.22
  631.6 2.7 collective-permute-start.23
  636.0 1.6 collective-permute-start.25
  648.3 1.8 place_bases.1
  650.1 11.9 %collective-permute-done.22.refs_9_ = bf16[4,64,512]{2,1,0:T(8,128)(2,1)} collective-permute-done((bf16[4,64,512]{2,1,0:T(8,128)(2,1)}, bf16[4,64,512]{2,1,0:T(8,128)(2,1)}, u32[]{:S(2)}, u32[]{:S(2)}) %collective-permute-start.22) | collective-permute-done | bytes 262176 | tf_op jit(solution)/shard_map/ppermute | solution.py:303
  662.0 5.6 collective-permute-done.23.refs_10_
  667.6 6.8 collective-permute-done.24.refs_11_
  674.5 6.0 collective-permute-done.25.refs_12_
  682.4 3.8 finish_slots.1
  (289 shorter events, 88.2 us)
Async XLA Ops:
  7.2 103.6 %all-gather.3.cloned.1.call-start = ((), (), s32[]{:S(2)}) async-start(), calls=%async_computation.4 | async-start | bytes 13516800 | tf_op jit(solution)/shard_map/all_gather | solution.py:782
  9.9 319.3 %reduce-scatter.3.cloned.1.call-start = ((), (), s32[]{:S(2)}) async-start(), calls=%async_computation.2 | async-start | bytes 15728640 | tf_op jit(solution)/shard_map/reduce_scatter | solution.py:963
  11.4 114.8 %copy-start.67 = (s32[72]{0:T(128)}, s32[72]{0:T(128)S(1)}, u32[]{:S(2)}) copy-start(s32[72]{0:T(128)S(1)} %pad_add_fusion.meta) | copy-start | bytes 868
  116.2 2.8 collective-permute-start
  119.2 2.8 collective-permute-start.1
  122.2 3.9 collective-permute-start.2
  137.2 2.8 collective-permute-start.3
  140.2 2.8 collective-permute-start.4
  143.2 3.8 collective-permute-start.5
  166.0 3.7 collective-permute-start.6
  170.6 2.9 collective-permute-start.7
  174.5 2.9 collective-permute-start.8
  201.1 3.7 collective-permute-start.9
  205.7 2.9 collective-permute-start.10
  209.6 2.8 collective-permute-start.11
  219.1 268.3 %reduce-scatter.5.cloned.1.call-start = ((), (), s32[]{:S(2)}) async-start(), calls=%async_computation.3 | async-start | bytes 4718592 | tf_op jit(solution)/shard_map/reduce_scatter | solution.py:967
  337.1 13.2 %collective-permute-start.12 = (bf16[6,64,512]{2,1,0:T(8,128)(2,1)S(1)}, bf16[6,64,512]{2,1,0:T(8,128)(2,1)S(1)}, u32[]{:S(2)}, u32[]{:S(2)}) collective-permute-start(bf16[6,64,512]{2,1,0:T(8,128)(2,1)S(1)} %get-tuple-element.104), channel_id=1, source_target_pairs={{0,4},{4,0},{8,12},{12,8},{16,20},{20,16},{24,28},{28,24},{1,5},{5... | collective-permute-start | bytes 1179656 | tf_op jit(solution)/shard_map/ppermute | solution.py:303
  338.3 30.8 %collective-permute-start.13 = (bf16[6,64,512]{2,1,0:T(8,128)(2,1)S(1)}, bf16[6,64,512]{2,1,0:T(8,128)(2,1)S(1)}, u32[]{:S(2)}, u32[]{:S(2)}) collective-permute-start(bf16[6,64,512]{2,1,0:T(8,128)(2,1)S(1)} %get-tuple-element.105), channel_id=1, source_target_pairs={{0,8},{4,12},{8,0},{12,4},{16,24},{20,28},{24,16},{28,20},{1,9},{5... | collective-permute-start | bytes 1179656 | tf_op jit(solution)/shard_map/ppermute | solution.py:303
  338.6 50.0 %collective-permute-start.14 = (bf16[6,64,512]{2,1,0:T(8,128)(2,1)S(1)}, bf16[6,64,512]{2,1,0:T(8,128)(2,1)S(1)}, u32[]{:S(2)}, u32[]{:S(2)}) collective-permute-start(bf16[6,64,512]{2,1,0:T(8,128)(2,1)S(1)} %get-tuple-element.106), channel_id=1, source_target_pairs={{0,12},{4,8},{8,4},{12,0},{16,28},{20,24},{24,20},{28,16},{1,13},{... | collective-permute-start | bytes 1179656 | tf_op jit(solution)/shard_map/ppermute | solution.py:303
  339.9 33.6 %collective-permute-start.33 = (f32[18,512]{1,0:T(8,128)S(1)}, f32[18,512]{1,0:T(8,128)S(1)}, u32[]{:S(2)}, u32[]{:S(2)}) collective-permute-start(f32[18,512]{1,0:T(8,128)S(1)} %pad_maximum_fusion), channel_id=1, source_target_pairs={{0,1},{1,0},{2,3},{3,2},{4,5},{5,4},{6,7},{7,6},{8,9},{9,8},{10,11... | collective-permute-start | bytes 110600 | tf_op jit(solution)/shard_map/ppermute | solution.py:330
  341.5 49.3 %collective-permute-start.15 = (bf16[6,64,512]{2,1,0:T(8,128)(2,1)S(1)}, bf16[6,64,512]{2,1,0:T(8,128)(2,1)S(1)}, u32[]{:S(2)}, u32[]{:S(2)}) collective-permute-start(bf16[6,64,512]{2,1,0:T(8,128)(2,1)S(1)} %get-tuple-element.107), channel_id=1, source_target_pairs={{0,16},{4,20},{8,24},{12,28},{16,0},{20,4},{24,8},{28,12},{1,17},{... | collective-permute-start | bytes 1179656 | tf_op jit(solution)/shard_map/ppermute | solution.py:303
  350.3 43.7 %collective-permute-start.16 = (bf16[6,64,512]{2,1,0:T(8,128)(2,1)S(1)}, bf16[6,64,512]{2,1,0:T(8,128)(2,1)S(1)}, u32[]{:S(2)}, u32[]{:S(2)}) collective-permute-start(bf16[6,64,512]{2,1,0:T(8,128)(2,1)S(1)} %get-tuple-element.108), channel_id=1, source_target_pairs={{0,20},{4,16},{8,28},{12,24},{16,4},{20,0},{24,12},{28,8},{1,21},{... | collective-permute-start | bytes 1179656 | tf_op jit(solution)/shard_map/ppermute | solution.py:303
  369.1 66.9 %collective-permute-start.17 = (bf16[6,64,512]{2,1,0:T(8,128)(2,1)S(1)}, bf16[6,64,512]{2,1,0:T(8,128)(2,1)S(1)}, u32[]{:S(2)}, u32[]{:S(2)}) collective-permute-start(bf16[6,64,512]{2,1,0:T(8,128)(2,1)S(1)} %get-tuple-element.109), channel_id=1, source_target_pairs={{0,24},{4,28},{8,16},{12,20},{16,8},{20,12},{24,0},{28,4},{1,25},{... | collective-permute-start | bytes 1179656 | tf_op jit(solution)/shard_map/ppermute | solution.py:303
  373.5 72.7 %collective-permute-start.18 = (bf16[6,64,512]{2,1,0:T(8,128)(2,1)S(1)}, bf16[6,64,512]{2,1,0:T(8,128)(2,1)S(1)}, u32[]{:S(2)}, u32[]{:S(2)}) collective-permute-start(bf16[6,64,512]{2,1,0:T(8,128)(2,1)S(1)} %get-tuple-element.110), channel_id=1, source_target_pairs={{0,28},{4,24},{8,20},{12,16},{16,12},{20,8},{24,4},{28,0},{1,29},{... | collective-permute-start | bytes 1179656 | tf_op jit(solution)/shard_map/ppermute | solution.py:303
  388.6 209.9 %collective-permute-start.34 = (f32[18,512]{1,0:T(8,128)}, f32[18,512]{1,0:T(8,128)}, u32[]{:S(2)}, u32[]{:S(2)}) collective-permute-start(f32[18,512]{1,0:T(8,128)} %fusion.24), channel_id=1, source_target_pairs={{0,2},{1,3},{2,0},{3,1},{4,6},{5,7},{6,4},{7,5},{8,10},{9,11},{10,... | collective-permute-start | bytes 110600 | tf_op jit(solution)/shard_map/ppermute | solution.py:330
  491.5 149.0 %copy-start.74 = (f32[288]{0:T(512)S(1)}, f32[288]{0:T(512)}, u32[]{:S(2)}) copy-start(f32[288]{0:T(512)} %param.21) | copy-start | bytes 3460
  491.5 149.0 %copy-start.76 = (f32[288]{0:T(512)S(1)}, f32[288]{0:T(512)}, u32[]{:S(2)}) copy-start(f32[288]{0:T(512)} %param.22) | copy-start | bytes 3460
  491.5 149.0 %copy-start.77 = (f32[288]{0:T(512)S(1)}, f32[288]{0:T(512)}, u32[]{:S(2)}) copy-start(f32[288]{0:T(512)} %param.23) | copy-start | bytes 3460
  500.8 179.6 %copy-start = (f32[6,2,64,512]{3,2,1,0:T(8,128)S(1)}, f32[6,2,64,512]{3,2,1,0:T(8,128)}, u32[]{:S(2)}) copy-start(f32[6,2,64,512]{3,2,1,0:T(8,128)} %refs_4_.1) | copy-start | bytes 4718596
  500.8 179.6 %copy-start.25 = (bf16[4,64,512]{2,1,0:T(8,128)(2,1)S(1)}, bf16[4,64,512]{2,1,0:T(8,128)(2,1)}, u32[]{:S(2)}) copy-start(bf16[4,64,512]{2,1,0:T(8,128)(2,1)} %copy-done.24) | copy-start | bytes 786436
  597.3 14.5 %collective-permute-start.26 = (bf16[2,64,512]{2,1,0:T(8,128)(2,1)S(1)}, bf16[2,64,512]{2,1,0:T(8,128)(2,1)S(1)}, u32[]{:S(2)}, u32[]{:S(2)}) collective-permute-start(bf16[2,64,512]{2,1,0:T(8,128)(2,1)S(1)} %get-tuple-element.125), channel_id=1, source_target_pairs={{0,4},{4,0},{8,12},{12,8},{16,20},{20,16},{24,28},{28,24},{1,5},{5... | collective-permute-start | bytes 393224 | tf_op jit(solution)/shard_map/ppermute | solution.py:303
  599.3 3.8 collective-permute-start.35
  603.1 3.0 collective-permute-start.36
  606.8 4.1 collective-permute-start.37
  607.9 4.8 collective-permute-start.27
  608.9 6.9 collective-permute-start.28
  610.1 6.6 collective-permute-start.29
  610.9 23.4 %collective-permute-start.19 = (bf16[4,64,512]{2,1,0:T(8,128)(2,1)S(1)}, bf16[4,64,512]{2,1,0:T(8,128)(2,1)S(1)}, u32[]{:S(2)}, u32[]{:S(2)}) collective-permute-start(bf16[4,64,512]{2,1,0:T(8,128)(2,1)S(1)} %get-tuple-element.112), channel_id=1, source_target_pairs={{0,4},{4,0},{8,12},{12,8},{16,20},{20,16},{24,28},{28,24},{1,5},{5... | collective-permute-start | bytes 786440 | tf_op jit(solution)/shard_map/ppermute | solution.py:303
  612.5 22.8 %collective-permute-start.20 = (bf16[4,64,512]{2,1,0:T(8,128)(2,1)S(1)}, bf16[4,64,512]{2,1,0:T(8,128)(2,1)S(1)}, u32[]{:S(2)}, u32[]{:S(2)}) collective-permute-start(bf16[4,64,512]{2,1,0:T(8,128)(2,1)S(1)} %get-tuple-element.113), channel_id=1, source_target_pairs={{0,8},{4,12},{8,0},{12,4},{16,24},{20,28},{24,16},{28,20},{1,9},{5... | collective-permute-start | bytes 786440 | tf_op jit(solution)/shard_map/ppermute | solution.py:303
  613.4 11.8 %collective-permute-start.30 = (bf16[2,64,512]{2,1,0:T(8,128)(2,1)S(1)}, bf16[2,64,512]{2,1,0:T(8,128)(2,1)S(1)}, u32[]{:S(2)}, u32[]{:S(2)}) collective-permute-start(bf16[2,64,512]{2,1,0:T(8,128)(2,1)S(1)} %get-tuple-element.129), channel_id=1, source_target_pairs={{0,20},{4,16},{8,28},{12,24},{16,4},{20,0},{24,12},{28,8},{1,21},{... | collective-permute-start | bytes 393224 | tf_op jit(solution)/shard_map/ppermute | solution.py:303
  616.5 9.3 %collective-permute-start.31 = (bf16[2,64,512]{2,1,0:T(8,128)(2,1)S(1)}, bf16[2,64,512]{2,1,0:T(8,128)(2,1)S(1)}, u32[]{:S(2)}, u32[]{:S(2)}) collective-permute-start(bf16[2,64,512]{2,1,0:T(8,128)(2,1)S(1)} %get-tuple-element.130), channel_id=1, source_target_pairs={{0,24},{4,28},{8,16},{12,20},{16,8},{20,12},{24,0},{28,4},{1,25},{... | collective-permute-start | bytes 393224 | tf_op jit(solution)/shard_map/ppermute | solution.py:303
  617.4 13.6 %collective-permute-start.32 = (bf16[2,64,512]{2,1,0:T(8,128)(2,1)S(1)}, bf16[2,64,512]{2,1,0:T(8,128)(2,1)S(1)}, u32[]{:S(2)}, u32[]{:S(2)}) collective-permute-start(bf16[2,64,512]{2,1,0:T(8,128)(2,1)S(1)} %get-tuple-element.131), channel_id=1, source_target_pairs={{0,28},{4,24},{8,20},{12,16},{16,12},{20,8},{24,4},{28,0},{1,29},{... | collective-permute-start | bytes 393224 | tf_op jit(solution)/shard_map/ppermute | solution.py:303
  625.8 24.3 %collective-permute-start.21 = (bf16[4,64,512]{2,1,0:T(8,128)(2,1)}, bf16[4,64,512]{2,1,0:T(8,128)(2,1)}, u32[]{:S(2)}, u32[]{:S(2)}) collective-permute-start(bf16[4,64,512]{2,1,0:T(8,128)(2,1)} %get-tuple-element.114), channel_id=1, source_target_pairs={{0,12},{4,8},{8,4},{12,0},{16,28},{20,24},{24,20},{28,16},{1,13},{... | collective-permute-start | bytes 786440 | tf_op jit(solution)/shard_map/ppermute | solution.py:303
  626.5 35.5 %collective-permute-start.22 = (bf16[4,64,512]{2,1,0:T(8,128)(2,1)}, bf16[4,64,512]{2,1,0:T(8,128)(2,1)}, u32[]{:S(2)}, u32[]{:S(2)}) collective-permute-start(bf16[4,64,512]{2,1,0:T(8,128)(2,1)} %get-tuple-element.115), channel_id=1, source_target_pairs={{0,16},{4,20},{8,24},{12,28},{16,0},{20,4},{24,8},{28,12},{1,17},{... | collective-permute-start | bytes 786440 | tf_op jit(solution)/shard_map/ppermute | solution.py:303
  631.6 36.0 %collective-permute-start.23 = (bf16[4,64,512]{2,1,0:T(8,128)(2,1)}, bf16[4,64,512]{2,1,0:T(8,128)(2,1)}, u32[]{:S(2)}, u32[]{:S(2)}) collective-permute-start(bf16[4,64,512]{2,1,0:T(8,128)(2,1)} %get-tuple-element.116), channel_id=1, source_target_pairs={{0,20},{4,16},{8,28},{12,24},{16,4},{20,0},{24,12},{28,8},{1,21},{... | collective-permute-start | bytes 786440 | tf_op jit(solution)/shard_map/ppermute | solution.py:303
  635.1 39.4 %collective-permute-start.24 = (bf16[4,64,512]{2,1,0:T(8,128)(2,1)}, bf16[4,64,512]{2,1,0:T(8,128)(2,1)}, u32[]{:S(2)}, u32[]{:S(2)}) collective-permute-start(bf16[4,64,512]{2,1,0:T(8,128)(2,1)} %get-tuple-element.117), channel_id=1, source_target_pairs={{0,24},{4,28},{8,16},{12,20},{16,8},{20,12},{24,0},{28,4},{1,25},{... | collective-permute-start | bytes 786440 | tf_op jit(solution)/shard_map/ppermute | solution.py:303
  636.0 44.5 %collective-permute-start.25 = (bf16[4,64,512]{2,1,0:T(8,128)(2,1)}, bf16[4,64,512]{2,1,0:T(8,128)(2,1)}, u32[]{:S(2)}, u32[]{:S(2)}) collective-permute-start(bf16[4,64,512]{2,1,0:T(8,128)(2,1)} %get-tuple-element.118), channel_id=1, source_target_pairs={{0,28},{4,24},{8,20},{12,16},{16,12},{20,8},{24,4},{28,0},{1,29},{... | collective-permute-start | bytes 786440 | tf_op jit(solution)/shard_map/ppermute | solution.py:303
  640.5 40.0 %copy-start.3 = (f32[6,64,512]{2,1,0:T(8,128)S(1)}, f32[6,64,512]{2,1,0:T(8,128)}, u32[]{:S(2)}) copy-start(f32[6,64,512]{2,1,0:T(8,128)} %refs_1_.1) | copy-start | bytes 2359300
  (71 other events, 191.5 us)
Sparse Core Ops, SparseCore 0:
  11.4 99.3 all-gather.2
  219.3 109.8 reduce-scatter.2
  333.7 153.7 reduce-scatter.4
